TPU v7x, 256 devices: a whole 4x4x8 slice. The times are simulated.
256 devices in a mesh: sta: 64 (over y, z_hi, x), win: 4 (over z_lo, core).
Axes of the slice: x: 4, y: 4, z: 8 (z_hi: 4, z_lo: 2; z = z_hi * 2 + z_lo), core: 2. Of those that a mesh axis runs over, the one named last changes fastest.
Arguments:
- records: bfloat16 [2048, 64, 2048], P('sta', 'win'), may hold values from -160 to 160
- gap_mask: int32 [2048, 64], P('sta', 'win'), may hold values from 0 to 1, as said below
Outputs:
- stacks: bfloat16 [3, 2048, 32, 2001], P(None, ('sta', 'win'))
Inputs may be any that keep to these rules, and one draw needn't show every extreme that they name: `gap_mask`: some channels have no valid window at all.
All inputs are finite; a program needn't handle non-finite values.
Results may differ from a plain program's by a relative error of at most 0.014.
Values may be sent and summed in bfloat16 or wider, within the bound.
No kernel may reach another device: no remote copies, remote signals or barrier semaphores. Data moves between devices by JAX's collectives and lax.ppermute only.
A program may use at most 128 MiB of HBM per device.

v0:
```python
import math

import jax
import jax.numpy as jnp
from jax import lax
from jax.sharding import PartitionSpec as P

SEG = 2048
NFFT = 4096
BINS = 512
SMOOTH = 4
LAGHALF = 1000
ROUNDS = 3
LAGS = 2001


def shifted(value, axis, steps):
    count = lax.axis_size(axis)
    pairs = [(source, (source + steps) % count) for source in range(count)]
    return lax.ppermute(value, axis, pairs)


def forward_table():
    samples = jnp.arange(SEG, dtype=jnp.int32)
    frequencies = jnp.arange(1, BINS + 1, dtype=jnp.int32)
    phases = samples[:, None] * frequencies[None, :] % NFFT
    angles = phases.astype(jnp.float32) * (2.0 * math.pi / NFFT)
    norm_scale = 1.0 / math.sqrt(SEG)
    return jnp.concatenate(
        [jnp.cos(angles) * norm_scale, -jnp.sin(angles) * norm_scale], axis=1
    ).astype(jnp.bfloat16)


def inverse_table():
    frequencies = jnp.arange(1, BINS + 1, dtype=jnp.int32)
    shifts = jnp.arange(LAGS, dtype=jnp.int32) - LAGHALF
    phases = frequencies[:, None] * shifts[None, :] % NFFT
    angles = phases.astype(jnp.float32) * (2.0 * math.pi / NFFT)
    norm_scale = math.sqrt(2.0 / BINS)
    return jnp.concatenate(
        [jnp.cos(angles) * norm_scale, -jnp.sin(angles) * norm_scale], axis=0
    ).astype(jnp.bfloat16)


def whitened_spectra(records, valid_rows, forward):
    signal = records.astype(jnp.float32)
    centred = signal - jnp.mean(signal, axis=-1, keepdims=True)
    spread = jnp.sqrt(jnp.mean(centred * centred, axis=-1, keepdims=True) + 1e-06)
    normal_rows = (centred / spread).astype(jnp.bfloat16)
    row_count, window_count = (records.shape[0], records.shape[1])
    spectrum = jnp.dot(
        normal_rows.reshape(row_count * window_count, SEG),
        forward,
        preferred_element_type=jnp.float32,
    )
    spectrum = spectrum.reshape(row_count, window_count, 2 * BINS)
    real_part = spectrum[..., :BINS]
    imag_part = spectrum[..., BINS:]
    power_sum = real_part * real_part + imag_part * imag_part
    padded = jnp.pad(power_sum, ((0, 0), (0, 0), (SMOOTH, SMOOTH)))
    filled = jnp.pad(jnp.ones((BINS,), jnp.float32), (SMOOTH, SMOOTH))
    window_sum = padded[..., 0:BINS]
    ones_sum = filled[0:BINS]
    for offset in range(1, 2 * SMOOTH + 1):
        window_sum = window_sum + padded[..., offset : offset + BINS]
        ones_sum = ones_sum + filled[offset : offset + BINS]
    smoothed = window_sum / ones_sum
    factor = 1.0 / jnp.sqrt(smoothed + 0.1)
    joined = jnp.concatenate([real_part * factor, imag_part * factor], axis=-1)
    return (joined * valid_rows[..., None]).astype(jnp.bfloat16)


def cross_spectra(own_spec, other_spec):
    own_real = own_spec[..., :BINS]
    own_imag = own_spec[..., BINS:]
    right_side = jnp.concatenate([other_spec[..., :BINS], other_spec[..., BINS:]], axis=1)
    left_real = jnp.concatenate([own_real, own_imag], axis=1)
    left_imag = jnp.concatenate([own_imag, -own_real], axis=1)
    real_sum = jnp.einsum("cwk,qwk->cqk", left_real, right_side, preferred_element_type=jnp.float32)
    imag_sum = jnp.einsum("cwk,qwk->cqk", left_imag, right_side, preferred_element_type=jnp.float32)
    return jnp.concatenate([real_sum, imag_sum], axis=-1)


def finish_pairs(summed, pair_count, inverse):
    row_count, partner_count = (summed.shape[0], summed.shape[1])
    low = summed.astype(jnp.bfloat16).reshape(row_count * partner_count, 2 * BINS)
    lagged = jnp.dot(low, inverse, preferred_element_type=jnp.float32).reshape(
        row_count, partner_count, LAGS
    )
    return (lagged / jnp.sqrt(jnp.maximum(pair_count, 1.0))[..., None]).astype(jnp.bfloat16)


def per_device(records, gap_mask):
    valid_rows = gap_mask.astype(jnp.float32)
    whitened = whitened_spectra(records, valid_rows, forward_table())
    carried = gap_mask.astype(jnp.bfloat16)
    inverse = inverse_table()
    partner_spec, partner_valid = (whitened, carried)
    results = []
    for round_index in range(ROUNDS):
        partner_spec, partner_valid = shifted((partner_spec, partner_valid), "sta", 1)
        cross_part = cross_spectra(whitened, partner_spec)
        paired = jnp.dot(
            valid_rows, partner_valid.astype(jnp.float32).T, preferred_element_type=jnp.float32
        )
        summed, pair_count = (
            lax.psum_scatter(
                cross_part.astype(jnp.bfloat16), "win", scatter_dimension=0, tiled=True
            ).astype(jnp.float32),
            lax.psum_scatter(
                paired.astype(jnp.bfloat16), "win", scatter_dimension=0, tiled=True
            ).astype(jnp.float32),
        )
        results.append(finish_pairs(summed, pair_count, inverse))
    return jnp.stack(results)


def solution(mesh):
    in_specs = (P("sta", "win", None), P("sta", "win"))
    out_specs = P(None, ("sta", "win"), None, None)
    return jax.shard_map(
        per_device, mesh=mesh, in_specs=in_specs, out_specs=out_specs, check_vma=False
    )
```

profile of v0, /device:TPU:128, one launch (start us, length us, event | category | flops | bytes accessed | tf_op | source)
XLA Modules:
  0.0 359.3 jit_solution(14969488648373962316)
XLA Ops:
  6.5 17.1 %multiply_convert_fusion.1 = (bf16[2048,512]{1,0:T(8,128)(2,1)S(1)}, bf16[2048,512]{1,0:T(8,128)(2,1)S(1)}) fusion(s32[512]{0:T(512)S(1)} %iota_add_fusion.1), kind=kLoop, calls=%fused_computation.22 | loop fusion | flops 19922944 | bytes 4196352 | tf_op jit(solution)/shard_map/convert.14
  23.7 0.3 convert_reduce_fusion
  24.0 0.7 fusion.2
  24.7 0.1 fusion.42
  24.8 2.4 fusion.7
  27.2 0.2 multiply_add_fusion
  27.4 2.2 slice_multiply_fusion.1
  29.7 0.2 slice_multiply_fusion
  29.9 0.1 copy.4
  30.0 0.2 fusion.23
  30.2 2.1 collective-permute-start
  32.3 0.1 fusion.52
  32.4 0.3 pad_maximum_fusion.5
  32.7 6.9 %copy.8 = bf16[32,32,512]{0,1,2:T(8,128)(2,1)} copy(bf16[32,32,512]{2,1,0:T(8,128)(2,1)S(1)} %get-tuple-element.20) | data formatting | bytes 2097152 | tf_op jit(solution)/shard_map/concatenate | solution.py:78
  39.5 6.8 %copy.6 = bf16[32,32,512]{0,1,2:T(8,128)(2,1)} copy(bf16[32,32,512]{2,1,0:T(8,128)(2,1)S(1)} %get-tuple-element.19) | data formatting | bytes 2097152 | tf_op jit(solution)/shard_map/concatenate | solution.py:77
  46.4 36.0 %collective-permute-done = bf16[32,16,1024]{2,1,0:T(8,128)(2,1)} collective-permute-done((bf16[32,16,1024]{2,1,0:T(8,128)(2,1)S(1)}, bf16[32,16,1024]{2,1,0:T(8,128)(2,1)}, u32[]{:S(2)}, u32[]{:S(2)}) %collective-permute-start) | collective-permute-done | bytes 1048608 | tf_op jit(solution)/shard_map/ppermute | solution.py:20
  82.4 1.3 fusion.50
  83.7 0.1 pad_maximum_fusion.4
  83.7 6.5 %copy.5 = bf16[32,32,512]{1,0,2:T(8,128)(2,1)} copy(bf16[32,32,512]{2,1,0:T(8,128)(2,1)S(1)} %pad_maximum_fusion.4) | data formatting | bytes 2097152 | tf_op jit(solution)/shard_map/concatenate | solution.py:76
  90.2 6.6 %fusion.56 = bf16[512,32,32]{2,1,0:T(8,128)(2,1)} fusion(bf16[32,32,512]{1,0,2:T(8,128)(2,1)} %copy.5, bf16[32,32,512]{0,1,2:T(8,128)(2,1)} %copy.8), kind=kOutput, calls=%fused_computation.121 | convolution fusion | flops 33554432 | bytes 3145728 | tf_op jit(solution)/shard_map/cwk,qwk->cqk/dot_general | solution.py:80
  96.8 5.2 %copy.9 = bf16[512,32,32]{0,1,2:T(8,128)(2,1)S(1)} copy(bf16[512,32,32]{2,1,0:T(8,128)(2,1)} %fusion.56) | data formatting | bytes 2097152 | tf_op jit(solution)/shard_map/cwk,qwk->cqk/dot_general | solution.py:80
  102.1 6.6 %fusion.55 = bf16[512,32,32]{2,1,0:T(8,128)(2,1)} fusion(bf16[32,32,512]{1,0,2:T(8,128)(2,1)} %copy.5, bf16[32,32,512]{0,1,2:T(8,128)(2,1)} %copy.6), kind=kOutput, calls=%fused_computation.120 | convolution fusion | flops 33554432 | bytes 3145728 | tf_op jit(solution)/shard_map/cwk,qwk->cqk/dot_general | solution.py:79
  108.7 5.2 %copy.7 = bf16[512,32,32]{0,1,2:T(8,128)(2,1)S(1)} copy(bf16[512,32,32]{2,1,0:T(8,128)(2,1)} %fusion.55) | data formatting | bytes 2097152 | tf_op jit(solution)/shard_map/cwk,qwk->cqk/dot_general | solution.py:79
  113.9 1.6 pad_maximum_fusion.1
  115.5 0.0 reduce-scatter.4.cloned.1.call-update
  115.6 0.0 reduce-scatter.6.cloned.1.call-start
  115.6 0.3 collective-permute-start.2
  115.9 68.4 %collective-permute-done.2 = bf16[32,16,1024]{2,1,0:T(8,128)(2,1)S(1)} collective-permute-done((bf16[32,16,1024]{2,1,0:T(8,128)(2,1)}, bf16[32,16,1024]{2,1,0:T(8,128)(2,1)S(1)}, u32[]{:S(2)}, u32[]{:S(2)}) %collective-permute-start.2) | collective-permute-done | bytes 1048608 | tf_op jit(solution)/shard_map/ppermute | solution.py:20
  184.3 0.1 fusion.51
  184.4 0.1 pad_maximum_fusion.7
  184.5 6.5 %copy.10 = bf16[32,32,512]{1,0,2:T(8,128)(2,1)} copy(bf16[32,32,512]{2,1,0:T(8,128)(2,1)S(1)} %pad_maximum_fusion.7) | data formatting | bytes 2097152 | tf_op jit(solution)/shard_map/concatenate | solution.py:76
  191.0 6.6 %fusion.58 = bf16[512,32,32]{2,1,0:T(8,128)(2,1)} fusion(bf16[32,32,512]{1,0,2:T(8,128)(2,1)} %copy.10, bf16[32,32,512]{0,1,2:T(8,128)(2,1)} %copy.8), kind=kOutput, calls=%fused_computation.123 | convolution fusion | flops 33554432 | bytes 3145728 | tf_op jit(solution)/shard_map/cwk,qwk->cqk/dot_general | solution.py:80
  197.6 5.2 %copy.12 = bf16[512,32,32]{0,1,2:T(8,128)(2,1)S(1)} copy(bf16[512,32,32]{2,1,0:T(8,128)(2,1)} %fusion.58) | data formatting | bytes 2097152 | tf_op jit(solution)/shard_map/cwk,qwk->cqk/dot_general | solution.py:80
  202.8 6.6 %fusion.57 = bf16[512,32,32]{2,1,0:T(8,128)(2,1)} fusion(bf16[32,32,512]{1,0,2:T(8,128)(2,1)} %copy.10, bf16[32,32,512]{0,1,2:T(8,128)(2,1)} %copy.6), kind=kOutput, calls=%fused_computation.122 | convolution fusion | flops 33554432 | bytes 3145728 | tf_op jit(solution)/shard_map/cwk,qwk->cqk/dot_general | solution.py:79
  209.5 5.2 %copy.11 = bf16[512,32,32]{0,1,2:T(8,128)(2,1)S(1)} copy(bf16[512,32,32]{2,1,0:T(8,128)(2,1)} %fusion.57) | data formatting | bytes 2097152 | tf_op jit(solution)/shard_map/cwk,qwk->cqk/dot_general | solution.py:79
  214.7 1.6 pad_maximum_fusion.2
  216.3 0.0 reduce-scatter.8.cloned.1.call-start
  216.4 0.3 collective-permute-start.4
  216.7 44.8 %collective-permute-done.4 = bf16[32,16,1024]{2,1,0:T(8,128)(2,1)S(1)} collective-permute-done((bf16[32,16,1024]{2,1,0:T(8,128)(2,1)S(1)}, bf16[32,16,1024]{2,1,0:T(8,128)(2,1)S(1)}, u32[]{:S(2)}, u32[]{:S(2)}) %collective-permute-start.4) | collective-permute-done | bytes 1048608 | tf_op jit(solution)/shard_map/ppermute | solution.py:20
  261.5 0.1 fusion.53
  261.6 0.1 pad_maximum_fusion.8
  261.7 6.5 %copy.13 = bf16[32,32,512]{1,0,2:T(8,128)(2,1)} copy(bf16[32,32,512]{2,1,0:T(8,128)(2,1)S(1)} %pad_maximum_fusion.8) | data formatting | bytes 2097152 | tf_op jit(solution)/shard_map/concatenate | solution.py:76
  268.1 6.6 %fusion.60 = bf16[512,32,32]{2,1,0:T(8,128)(2,1)} fusion(bf16[32,32,512]{1,0,2:T(8,128)(2,1)} %copy.13, bf16[32,32,512]{0,1,2:T(8,128)(2,1)} %copy.8), kind=kOutput, calls=%fused_computation.125 | convolution fusion | flops 33554432 | bytes 3145728 | tf_op jit(solution)/shard_map/cwk,qwk->cqk/dot_general | solution.py:80
  274.8 5.2 %copy.15 = bf16[512,32,32]{0,1,2:T(8,128)(2,1)S(1)} copy(bf16[512,32,32]{2,1,0:T(8,128)(2,1)} %fusion.60) | data formatting | bytes 2097152 | tf_op jit(solution)/shard_map/cwk,qwk->cqk/dot_general | solution.py:80
  280.0 6.7 %fusion.59 = bf16[512,32,32]{2,1,0:T(8,128)(2,1)} fusion(bf16[32,32,512]{1,0,2:T(8,128)(2,1)} %copy.13, bf16[32,32,512]{0,1,2:T(8,128)(2,1)} %copy.6), kind=kOutput, calls=%fused_computation.124 | convolution fusion | flops 33554432 | bytes 3145728 | tf_op jit(solution)/shard_map/cwk,qwk->cqk/dot_general | solution.py:79
  286.7 5.2 %copy.14 = bf16[512,32,32]{0,1,2:T(8,128)(2,1)S(1)} copy(bf16[512,32,32]{2,1,0:T(8,128)(2,1)} %fusion.59) | data formatting | bytes 2097152 | tf_op jit(solution)/shard_map/cwk,qwk->cqk/dot_general | solution.py:79
  291.9 1.6 pad_maximum_fusion.3
  293.5 0.0 reduce-scatter.8.cloned.1.call-update
  293.5 0.1 collective-permute-start.1
  293.6 18.5 %multiply_convert_fusion.3 = (bf16[512,2001]{0,1:T(8,128)(2,1)S(1)}, bf16[512,2001]{0,1:T(8,128)(2,1)}) fusion(s32[2001]{0:T(1024)S(1)} %iota_add_fusion, s32[512]{0:T(512)S(1)} %iota_add_fusion.1), kind=kLoop, calls=%fused_computation.31 | loop fusion | flops 19465728 | bytes 4108100 | tf_op jit(solution)/shard_map/convert.8
  312.1 0.6 dynamic-slice
  313.5 0.1 collective-permute-start.3
  313.6 0.2 convolution_convert_fusion.2
  313.7 7.9 %collective-permute-done.3 = bf16[32,16]{0,1:T(8,128)(2,1)S(1)} collective-permute-done((bf16[32,16]{0,1:T(8,128)(2,1)S(1)}, bf16[32,16]{0,1:T(8,128)(2,1)S(1)}, u32[]{:S(2)}, u32[]{:S(2)}) %collective-permute-start.3) | collective-permute-done | bytes 1056 | tf_op jit(solution)/shard_map/ppermute | solution.py:20
  321.6 0.2 convolution_convert_fusion.1
  321.8 7.6 %collective-permute-done.5 = bf16[32,16]{0,1:T(8,128)(2,1)S(1)} collective-permute-done((bf16[32,16]{0,1:T(8,128)(2,1)S(1)}, bf16[32,16]{0,1:T(8,128)(2,1)S(1)}, u32[]{:S(2)}, u32[]{:S(2)}) %collective-permute-start.5) | collective-permute-done | bytes 1056 | tf_op jit(solution)/shard_map/ppermute | solution.py:20
  329.5 0.2 convolution_convert_fusion
  329.6 10.6 %all-reduce.5 = (bf16[32,32]{1,0:T(8,128)(2,1)S(1)}, bf16[32,32]{1,0:T(8,128)(2,1)S(1)}, bf16[32,32]{1,0:T(8,128)(2,1)S(1)}) all-reduce(bf16[32,32]{1,0:T(8,128)(2,1)S(1)} %convolution_convert_fusion, bf16[32,32]{1,0:T(8,128)(2,1)S(1)} %convolution_convert_fusion.1, ...), channel_id=7, replica_groups=mesh['sta'=64,'win'=4] {'win'}, use_global_device_ids=true, to_apply=%region_7.8.clone | all-reduce | flops 3072 | bytes 12288
  340.2 0.0 reduce-scatter.4.cloned.1.call-done
  340.3 3.0 fusion.21
  343.3 0.0 reduce-scatter.6.cloned.1.call-done
  343.3 4.0 %fusion.19 = bf16[1,8,32,2001]{3,2,1,0:T(8,128)(2,1)} fusion(bf16[8,32,1024]{2,1,0:T(8,128)(2,1)} %reduce-scatter.6.cloned.1.call-done, bf16[512,2001]{0,1:T(8,128)(2,1)} %get-tuple-element.22, bf16[512,2001]{0,1:T(8,128)(2,1)S(1)} %get-tuple-element.21, f32[8,32]{1,0:T(8,128)S(1)} %get-tuple-element.28), kind=kOutput, calls=%fused_computation.38 | convolution fusion | flops 1058320896 | bytes 5647872 | tf_op jit(solution)/shard_map/dot_general | solution.py:87
  347.4 3.1 fusion.17
  350.5 2.0 pad_maximum_fusion
  (21 shorter events, 0.1 us)
Async XLA Ops:
  6.5 17.1 %copy-start = (bf16[32,16,2048]{2,1,0:T(8,128)(2,1)S(1)}, bf16[32,16,2048]{2,1,0:T(8,128)(2,1)}, u32[]{:S(2)}) copy-start(bf16[32,16,2048]{2,1,0:T(8,128)(2,1)} %param.2) | copy-start | bytes 6291460
  6.5 333.7 %reduce-scatter.4.cloned.1.call-start = ((), (), s32[]{:S(2)}) async-start(), calls=%async_computation.3 | async-start | bytes 2621440 | tf_op jit(solution)/shard_map/reduce_scatter | solution.py:107
  27.4 2.5 copy-start.2
  30.2 52.2 %collective-permute-start = (bf16[32,16,1024]{2,1,0:T(8,128)(2,1)S(1)}, bf16[32,16,1024]{2,1,0:T(8,128)(2,1)}, u32[]{:S(2)}, u32[]{:S(2)}) collective-permute-start(bf16[32,16,1024]{2,1,0:T(8,128)(2,1)S(1)} %fusion.23), channel_id=1, source_target_pairs={{0,4},{4,8},{8,12},{12,16},{16,20},{20,24},{24,28},{28,32},{32,36}... | collective-permute-start | bytes 3145736 | tf_op jit(solution)/shard_map/ppermute | solution.py:20
  115.6 227.8 %reduce-scatter.6.cloned.1.call-start = ((), (), s32[]{:S(2)}) async-start(), calls=%async_computation.4 | async-start | bytes 2621440 | tf_op jit(solution)/shard_map/reduce_scatter | solution.py:107
  115.6 68.7 %collective-permute-start.2 = (bf16[32,16,1024]{2,1,0:T(8,128)(2,1)}, bf16[32,16,1024]{2,1,0:T(8,128)(2,1)S(1)}, u32[]{:S(2)}, u32[]{:S(2)}) collective-permute-start(bf16[32,16,1024]{2,1,0:T(8,128)(2,1)} %collective-permute-done), channel_id=1, source_target_pairs={{0,4},{4,8},{8,12},{12,16},{16,20},{20,24},{24,28},{28,32},{32,36}... | collective-permute-start | bytes 3145736 | tf_op jit(solution)/shard_map/ppermute | solution.py:20
  216.3 131.1 %reduce-scatter.8.cloned.1.call-start = ((), (), s32[]{:S(2)}) async-start(), calls=%async_computation.5 | async-start | bytes 2621440 | tf_op jit(solution)/shard_map/reduce_scatter | solution.py:107
  216.4 45.1 %collective-permute-start.4 = (bf16[32,16,1024]{2,1,0:T(8,128)(2,1)S(1)}, bf16[32,16,1024]{2,1,0:T(8,128)(2,1)S(1)}, u32[]{:S(2)}, u32[]{:S(2)}) collective-permute-start(bf16[32,16,1024]{2,1,0:T(8,128)(2,1)S(1)} %collective-permute-done.2), channel_id=1, source_target_pairs={{0,4},{4,8},{8,12},{12,16},{16,20},{20,24},{24,28},{28,32},{32,36}... | collective-permute-start | bytes 3145736 | tf_op jit(solution)/shard_map/ppermute | solution.py:20
  293.5 18.6 %copy-start.3 = (u32[256]{0:T(256)S(1)}, u32[256]{0:T(256)}, u32[]{:S(2)}) copy-start(u32[256]{0:T(256)} %constant.59) | copy-start | bytes 3076
  293.5 19.9 %collective-permute-start.1 = (bf16[32,16]{0,1:T(8,128)(2,1)S(1)}, bf16[32,16]{0,1:T(8,128)(2,1)S(1)}, u32[]{:S(2)}, u32[]{:S(2)}) collective-permute-start(bf16[32,16]{0,1:T(8,128)(2,1)S(1)} %get-tuple-element.23), channel_id=1, source_target_pairs={{0,4},{4,8},{8,12},{12,16},{16,20},{20,24},{24,28},{28,32},{32,36}... | collective-permute-start | bytes 3080 | tf_op jit(solution)/shard_map/ppermute | solution.py:20
  313.5 8.2 %collective-permute-start.3 = (bf16[32,16]{0,1:T(8,128)(2,1)S(1)}, bf16[32,16]{0,1:T(8,128)(2,1)S(1)}, u32[]{:S(2)}, u32[]{:S(2)}) collective-permute-start(bf16[32,16]{0,1:T(8,128)(2,1)S(1)} %collective-permute-done.1), channel_id=1, source_target_pairs={{0,4},{4,8},{8,12},{12,16},{16,20},{20,24},{24,28},{28,32},{32,36}... | collective-permute-start | bytes 3080 | tf_op jit(solution)/shard_map/ppermute | solution.py:20
  321.6 7.8 %collective-permute-start.5 = (bf16[32,16]{0,1:T(8,128)(2,1)S(1)}, bf16[32,16]{0,1:T(8,128)(2,1)S(1)}, u32[]{:S(2)}, u32[]{:S(2)}) collective-permute-start(bf16[32,16]{0,1:T(8,128)(2,1)S(1)} %collective-permute-done.3), channel_id=1, source_target_pairs={{0,4},{4,8},{8,12},{12,16},{16,20},{20,24},{24,28},{28,32},{32,36}... | collective-permute-start | bytes 3080 | tf_op jit(solution)/shard_map/ppermute | solution.py:20
  347.4 3.1 copy-start.1
Sparse Core Ops, SparseCore 0:
  115.7 28.9 reduce-scatter.3
  216.4 28.9 reduce-scatter.5
  293.7 28.9 reduce-scatter.7
where the time goes:
time: 366 us; the launch traced here: 359 us
  waiting for transfers between devices  165 us (45%)
  local copies, waits for them, and re-layouts  66.8 us (18%)
  matrix products  52.9 us (14%)
  other arithmetic  47 us (13%)
  between operations  14.4 us (4%)
  blocking collectives  10.6 us (3%)
    ppermute x6, waiting for transfers between devices, shifted(): return lax.ppermute(value, axis, pairs)  165 us
    another operation x2, other arithmetic  35.6 us
    dot_general x3, matrix products, cross_spectra(): jnp.einsum('cwk,qwk->cqk', left_real, right_side, preferred_element_type=...  19.9 us
    dot_general x3, matrix products, cross_spectra(): jnp.einsum('cwk,qwk->cqk', left_imag, right_side, preferred_element_type=...  19.9 us
    concatenate x3, local copies, waits for them, and re-layouts, cross_spectra(): jnp.concatenate([other_spec[..., :BINS], other_spec[..., BINS:]], axis=1)  19.4 us
    dot_general x3, local copies, waits for them, and re-layouts, cross_spectra(): jnp.einsum('cwk,qwk->cqk', left_imag, right_side, preferred_element_type=...  15.7 us
    dot_general x3, local copies, waits for them, and re-layouts, cross_spectra(): jnp.einsum('cwk,qwk->cqk', left_real, right_side, preferred_element_type=...  15.7 us
    unnamed x1, blocking collectives  10.6 us
  transfers between devices with their start and end apart: 9, of which 5 were waited for; matrix products, arithmetic and copies ran while one was open for 29% of the time, Pallas kernels for 0%

commit v1 on v0

v1 whole, which is shorter than its diff:
```python
import functools
import math

import jax
import jax.numpy as jnp
import numpy as np
from jax import lax
from jax.experimental import pallas as pl
from jax.experimental.pallas import tpu as pltpu
from jax.sharding import Mesh, PartitionSpec as P

SEG = 2048
NFFT = 4096
BINS = 512
SMOOTH = 4
LAGHALF = 1000
LAGS = 2001
CH = 32
WIN = 16
BF = jnp.bfloat16
F32 = jnp.float32
PARTS = 1
NB = BINS // 16 // PARTS
PART_ROWS = 8 * NB
MASK_ROW = PARTS * PART_ROWS
SENT_ROWS = MASK_ROW + 8
GROUP = ("x", "zl", "core")
STATIONS = ("y", "zh", "x")


def forward_table():
    phases = np.arange(1, BINS + 1)[:, None] * np.arange(SEG)[None, :] % NFFT
    angles = phases * (2.0 * math.pi / NFFT)
    table = np.concatenate([np.cos(angles), -np.sin(angles)], axis=0) / math.sqrt(SEG)
    return table.astype(np.float32).astype(jnp.bfloat16)


def inverse_table():
    phases = np.arange(1, BINS + 1)[:, None] * (np.arange(LAGS) - LAGHALF)[None, :] % NFFT
    angles = phases * (2.0 * math.pi / NFFT)
    table = np.stack([np.cos(angles), -np.sin(angles)], axis=0) * math.sqrt(2.0 / BINS)
    table = table.reshape(2, 16, PARTS, NB, LAGS).transpose(2, 1, 0, 3, 4)
    return table.reshape(2 * BINS, LAGS).astype(np.float32).astype(jnp.bfloat16)


def nt_dot(a, b):
    return lax.dot_general(a, b, (((1,), (1,)), ((), ())), preferred_element_type=F32)


def tn_dot(a, b):
    return lax.dot_general(a, b, (((0,), (0,)), ((), ())), preferred_element_type=F32)


def spectra_kernel(rec, table, mask, out, planes, rows, spec, power):
    for c in range(0, CH, 4):
        signal = rec[c : c + 4].astype(F32).reshape(4 * WIN, SEG)
        centred = signal - jnp.mean(signal, axis=-1, keepdims=True)
        spread = jnp.sqrt(jnp.mean(centred * centred, axis=-1, keepdims=True) + 1e-06)
        normal = centred / spread
        for t in range(SEG // 128):
            planes[t, c * WIN : (c + 4) * WIN, :] = normal[:, t * 128 : (t + 1) * 128]
    for w in range(WIN):
        for t in range(SEG // 128):
            rows[w * CH : (w + 1) * CH, t * 128 : (t + 1) * 128] = planes[
                t, pl.ds(w, CH, stride=WIN), :
            ].astype(BF)

    def multiply(i, carry):
        at = pl.ds(pl.multiple_of(i * 256, 256), 256)
        spec[at, :] = nt_dot(table[at, :], rows[...])
        return carry

    lax.fori_loop(0, 4, multiply, 0)
    power[0:8, :] = jnp.zeros((8, 512), F32)
    power[8 + BINS : 16 + BINS, :] = jnp.zeros((8, 512), F32)
    for k in range(0, BINS, 64):
        real, imag = spec[k : k + 64, :], spec[BINS + k : BINS + k + 64, :]
        power[8 + k : 72 + k, :] = real * real + imag * imag
    window = lax.broadcasted_iota(jnp.int32, (WIN, 512), 0)
    pick = (lax.broadcasted_iota(jnp.int32, (WIN, 512), 1) // CH == window).astype(BF)
    spread = jnp.dot(mask[...].astype(F32).astype(BF), pick, preferred_element_type=F32)
    channel = lax.broadcasted_iota(jnp.int32, (CH, 512), 0)
    own_lane = lax.broadcasted_iota(jnp.int32, (CH, 512), 1) % CH == channel
    valid = jnp.sum(jnp.where(own_lane, spread, 0.0), axis=0, keepdims=True)
    sent_mask = jnp.concatenate(
        [valid[:, i * 128 : (i + 1) * 128] for i in range(4)] + [jnp.zeros((4, 128), F32)], axis=0
    ).astype(BF)
    step = NB * PARTS
    for dst in range(16):
        k = dst * step
        total = power[4 + k : 4 + k + step, :]
        for offset in range(1, 2 * SMOOTH + 1):
            total = total + power[4 + k + offset : 4 + k + offset + step, :]
        bins = k + lax.broadcasted_iota(jnp.int32, (step, 512), 0)
        count = jnp.minimum(bins, SMOOTH) + jnp.minimum(BINS - 1 - bins, SMOOTH) + 1
        factor = valid / jnp.sqrt(total / count.astype(F32) + 0.1)
        for ri in range(2):
            white = (spec[ri * BINS + k : ri * BINS + k + step, :] * factor).astype(BF)
            for part in range(PARTS):
                for high in range(4):
                    at = part * PART_ROWS + (high * 2 + ri) * NB
                    out[dst, at : at + NB, :] = white[
                        part * NB : (part + 1) * NB, high * 128 : (high + 1) * 128
                    ]
        out[dst, MASK_ROW:SENT_ROWS, :] = sent_mask


def spectra(records, gap_mask):
    full = pl.BlockSpec(memory_space=pltpu.VMEM)
    return pl.pallas_call(
        spectra_kernel,
        out_shape=jax.ShapeDtypeStruct((16, SENT_ROWS, 128), BF),
        in_specs=[full] * 3,
        out_specs=full,
        scratch_shapes=[
            pltpu.VMEM((SEG // 128, 512, 128), F32),
            pltpu.VMEM((512, SEG), BF),
            pltpu.VMEM((2 * BINS, 512), F32),
            pltpu.VMEM((BINS + 16, 512), F32),
        ],
        compiler_params=pltpu.CompilerParams(vmem_limit_bytes=48 << 20),
        cost_estimate=pl.CostEstimate(flops=2 * 512 * SEG * 2 * BINS, bytes_accessed=8 << 20, transcendentals=0),
        name="spectra",
    )(records, jnp.asarray(forward_table()), gap_mask)


def blocks_to_lanes(parts):
    lane = lax.broadcasted_iota(jnp.int32, parts[0].shape, 1)
    low, odd = lane < 64, (lane // 32) % 2 == 0
    half = []
    a0, a1, a2, a3 = parts
    half = [
        jnp.where(low, a0, pltpu.roll(a2, 64, 1)),
        jnp.where(low, a1, pltpu.roll(a3, 64, 1)),
        jnp.where(low, pltpu.roll(a0, 64, 1), a2),
        jnp.where(low, pltpu.roll(a1, 64, 1), a3),
    ]
    return [
        jnp.where(odd, half[0], pltpu.roll(half[1], 32, 1)),
        jnp.where(odd, pltpu.roll(half[0], 96, 1), half[1]),
        jnp.where(odd, half[2], pltpu.roll(half[3], 32, 1)),
        jnp.where(odd, pltpu.roll(half[2], 96, 1), half[3]),
    ]


def cross_kernel(part, own, prev, out, planes, pairs):
    for block in range(7):
        for v in range(4):
            for ri in range(2):
                source, first = (
                    (prev.at[block * 4 + v], 0)
                    if block < 3
                    else (own.at[(block - 3) * 4 + v], part * PART_ROWS)
                )
                for high in range(4):
                    row = ((block * 2 + ri) * 4 + v) * 4 + high
                    at = first + (high * 2 + ri) * NB
                    planes[row * NB : (row + 1) * NB, :] = source[at : at + NB, :].astype(F32)
    lane = lax.broadcasted_iota(jnp.int32, (32, 128), 1)

    def one_bin(k, carry):
        def side(blocks):
            found = []
            for ri in range(2):
                parts = [
                    planes[pl.ds((block * 2 + ri) * 16 * NB + k, 16, stride=NB), :] for block in blocks
                ]
                found.append(jnp.concatenate(blocks_to_lanes(parts), axis=0))
            return found

        prev_real, prev_imag = side((0, 0, 1, 2))
        own_real, own_imag = side((3, 4, 5, 6))
        left = jnp.concatenate(
            [
                jnp.concatenate([own_real, own_imag], axis=0),
                jnp.concatenate([own_imag, -own_real], axis=0),
            ],
            axis=1,
        ).astype(BF)
        right = jnp.concatenate(
            [
                jnp.concatenate([prev_real, prev_imag], axis=0),
                jnp.concatenate([own_real, own_imag], axis=0),
            ],
            axis=1,
        ).astype(BF)
        product = tn_dot(left, right)
        for ri in range(2):
            for b in range(4):
                at = ri * 128 + b * 32
                first, second = product[at : at + 32, :128], product[at : at + 32, 128:]
                if b == 3:
                    value = second
                else:
                    value = pltpu.roll(first, 96 - 32 * b, 1)
                    if b:
                        value = jnp.where(lane < 96 - 32 * b, value, pltpu.roll(second, 96 - 32 * b, 1))
                pairs[pl.ds(at * NB + k, 32, stride=NB), :] = value
        return carry

    lax.fori_loop(0, NB, one_bin, 0, unroll=4)
    lanes = lax.broadcasted_iota(jnp.int32, (NB, 128), 1)
    for ri in range(2):
        for b in range(4):
            for v in range(4):
                for high in range(2):
                    row = ri * 128 + b * 32 + v * 8 + high * 4
                    p0, p1, p2, p3 = [pairs[(row + i) * NB : (row + i + 1) * NB, :] for i in range(4)]
                    p1, p2, p3 = pltpu.roll(p1, 96, 1), pltpu.roll(p2, 64, 1), pltpu.roll(p3, 32, 1)
                    target = out.at[b * 4 + v, ri, high]
                    target[:, 0:128] = jnp.where(lanes < 96, p0, p1).astype(BF)
                    target[:, 128:256] = jnp.where(lanes < 64, p1, p2).astype(BF)
                    target[:, 256:384] = jnp.where(lanes < 32, p2, p3).astype(BF)


def cross(part, own, prev):
    full = pl.BlockSpec(memory_space=pltpu.VMEM)
    return pl.pallas_call(
        functools.partial(cross_kernel, part),
        out_shape=jax.ShapeDtypeStruct((16, 2, 2, NB, 384), BF),
        in_specs=[full] * 2,
        out_specs=full,
        scratch_shapes=[
            pltpu.VMEM((7 * 32 * NB, 128), F32),
            pltpu.VMEM((256 * NB, 128), F32),
        ],
        compiler_params=pltpu.CompilerParams(vmem_limit_bytes=48 << 20),
        cost_estimate=pl.CostEstimate(flops=(8 << 30) // PARTS, bytes_accessed=(4 << 20) // PARTS, transcendentals=0),
        name="cross",
    )(own, prev)


def lag_kernel(*refs):
    crosses, (table, own_mask, partner_mask, out) = refs[:PARTS], refs[PARTS:]
    count = nt_dot(partner_mask[...], own_mask[...])
    scale = 1.0 / jnp.sqrt(jnp.maximum(count, 1.0))
    for high in range(2):
        left = jnp.concatenate(
            [value[:, :, high].reshape(2 * BINS // PARTS, 384) for value in crosses], axis=0
        )
        turned = left.T
        for at in range(0, LAGS, 512):
            end = min(at + 512, LAGS)
            lagged = jnp.dot(turned, table[:, at:end], preferred_element_type=F32)
            for low in range(4):
                c = high * 4 + low
                for s in range(3):
                    row = low * 96 + s * 32
                    out[2 - s, c, :, at:end] = (
                        lagged[row : row + 32] * scale[s * 32 : s * 32 + 32, c : c + 1]
                    ).astype(BF)


def lag_sums(crosses, own_mask, partner_mask):
    full = pl.BlockSpec(memory_space=pltpu.VMEM)
    return pl.pallas_call(
        lag_kernel,
        out_shape=jax.ShapeDtypeStruct((3, 8, CH, LAGS), BF),
        in_specs=[full] * (PARTS + 3),
        out_specs=full,
        compiler_params=pltpu.CompilerParams(vmem_limit_bytes=48 << 20),
        cost_estimate=pl.CostEstimate(flops=2 * 768 * 2 * BINS * LAGS, bytes_accessed=9 << 20, transcendentals=0),
        name="lag_sums",
    )(*crosses, jnp.asarray(inverse_table()), own_mask, partner_mask)


def shifted(value, axes, count, steps):
    return lax.ppermute(value, axes, [(i, (i + steps) % count) for i in range(count)])


def from_previous_group(value):
    return shifted(value, ("y", "zh"), 16, 1)


def per_device(records, gap_mask):
    own = lax.all_to_all(spectra(records, gap_mask), GROUP, 0, 0, tiled=True)
    edges = [p * PART_ROWS for p in range(PARTS)] + [SENT_ROWS]
    prevs = [from_previous_group(own[4:, edges[p] : edges[p + 1]]) for p in range(PARTS)]
    crosses = [
        lax.all_to_all(cross(p, own, prevs[p]), GROUP, 0, 0, tiled=True) for p in range(PARTS)
    ]
    masks = jnp.concatenate([prevs[-1][:, PART_ROWS : PART_ROWS + 4], own[:, MASK_ROW : MASK_ROW + 4]], axis=0)
    masks = lax.dynamic_slice_in_dim(masks, lax.axis_index("x") * 4, 16, 0)
    masks = masks.reshape(4, 16, 4, CH).transpose(0, 3, 1, 2).reshape(4 * CH, 64)
    own_mask = lax.dynamic_slice_in_dim(masks, 3 * CH + lax.axis_index(("zl", "core")) * 8, 8, 0)
    return lag_sums(crosses, own_mask, masks[: 3 * CH])


def solution(mesh):
    fine = Mesh(mesh.devices.reshape(4, 4, 4, 2, 2), ("y", "zh", "x", "zl", "core"))
    in_specs = (P(("y", "zh", "x"), ("zl", "core"), None), P(("y", "zh", "x"), ("zl", "core")))
    out_specs = P(None, ("y", "zh", "x", "zl", "core"), None, None)
    return jax.shard_map(
        per_device, mesh=fine, in_specs=in_specs, out_specs=out_specs, check_vma=False
    )
```

time: 366 us -> 124 us (0.34)
  the two profiles are of different devices: /device:TPU:128 before, /device:TPU:1 now
where the time goes in v1:
time: 124 us
  waiting for transfers between devices  61.1 us (49%)
  Pallas kernels  24.9 us (20%)
  blocking collectives  23.6 us (19%)
  starting transfers between devices  7.48 us (6%)
  local copies, waits for them, and re-layouts  6.43 us (5%)
    ppermute x1, waiting for transfers between devices, shifted(): lax.ppermute(value, axes, [(i, (i + steps) % count) for i in range(count)])  40.3 us
    all_to_all x1, blocking collectives, per_device(): own = lax.all_to_all(spectra(records, gap_mask), GROUP, 0, 0, tiled=True)  23.6 us
    all_to_all x1, waiting for transfers between devices, per_device(): lax.all_to_all(cross(p, own, prevs[p]), GROUP, 0, 0, tiled=True)  20.7 us
    pallas_call x1, Pallas kernels, spectra(): pl.pallas_call(spectra_kernel, out_shape=jax.ShapeDtypeStruct((16, SENT_R...  10.4 us
    pallas_call x1, Pallas kernels, cross(): pl.pallas_call(functools.partial(cross_kernel, part), out_shape=jax.Shape...  9.38 us
    unnamed x8, local copies, waits for them, and re-layouts  5.76 us
    pallas_call x1, Pallas kernels, lag_sums(): pl.pallas_call(lag_kernel, out_shape=jax.ShapeDtypeStruct((3, 8, CH, LAGS...  5.1 us
    all_to_all x1, starting transfers between devices, per_device(): lax.all_to_all(cross(p, own, prevs[p]), GROUP, 0, 0, tiled=True)  4.41 us
  transfers between devices with their start and end apart: 2, of which 2 were waited for; matrix products, arithmetic and copies ran while one was open for 1% of the time, Pallas kernels for 0%

profile of v1, /device:TPU:1, one launch (start us, length us, event | category | flops | bytes accessed | tf_op | source)
XLA Modules:
  0.0 123.7 jit_solution(11621589139976290508)
XLA Ops:
  0.0 0.8 copy.6.mask
  0.8 0.0 copy-start.1
  0.8 1.6 %copy-done.1 = bf16[32,16,2048]{2,1,0:T(8,128)(2,1)S(1)} copy-done((bf16[32,16,2048]{2,1,0:T(8,128)(2,1)S(1)}, bf16[32,16,2048]{2,1,0:T(8,128)(2,1)}, u32[]{:S(2)}) %copy-start.1) | copy-done | bytes 2097176
  2.4 10.4 %spectra.1 = bf16[16,264,128]{2,1,0:T(8,128)(2,1)S(1)} custom-call(bf16[32,16,2048]{2,1,0:T(8,128)(2,1)S(1)} %copy-done.1, bf16[1024,2048]{1,0:T(8,128)(2,1)} %constant.30.clone.table, s32[32,16]{1,0:T(8,128)S(1)} %copy.6.mask), custom_call_target="tpu_custom_call" | custom-call | flops 2147483648 | bytes 8388608 | tf_op jit(solution)/shard_map/spectra/pallas_call | solution.py:110
  12.8 23.6 %all_to_all.10.own = bf16[16,264,128]{2,1,0:T(8,128)(2,1)S(1)} all-to-all(bf16[16,264,128]{2,1,0:T(8,128)(2,1)S(1)} %spectra.1), channel_id=1, replica_groups=mesh['y'=4,'zh'=4,'x'=4,'zl'=2,'core'=2] {'x','zl','core'}, dimensions={0} | all-to-all | bytes 2162688 | tf_op jit(solution)/shard_map/all_to_all | solution.py:276
  36.4 0.1 slice.20
  36.5 3.1 %collective-permute-start = (bf16[12,264,128]{2,1,0:T(8,128)(2,1)S(1)}, bf16[12,264,128]{2,1,0:T(8,128)(2,1)S(1)}, u32[]{:S(2)}, u32[]{:S(2)}) collective-permute-start(bf16[12,264,128]{2,1,0:T(8,128)(2,1)S(1)} %slice.20), channel_id=1, source_target_pairs={{0,16},{16,32},{32,48},{48,64},{64,80},{80,96},{96,112},{112,128},... | collective-permute-start | bytes 2433032 | tf_op jit(solution)/shard_map/ppermute | solution.py:268
  39.6 40.3 %collective-permute-done.prev = bf16[12,264,128]{2,1,0:T(8,128)(2,1)S(1)} collective-permute-done((bf16[12,264,128]{2,1,0:T(8,128)(2,1)S(1)}, bf16[12,264,128]{2,1,0:T(8,128)(2,1)S(1)}, u32[]{:S(2)}, u32[]{:S(2)}) %collective-permute-start) | collective-permute-done | bytes 811040 | tf_op jit(solution)/shard_map/ppermute | solution.py:268
  79.9 9.4 %cross.1 = bf16[16,2,2,32,384]{4,3,2,1,0:T(8,128)(2,1)S(1)} custom-call(bf16[16,264,128]{2,1,0:T(8,128)(2,1)S(1)} %all_to_all.10.own, bf16[12,264,128]{2,1,0:T(8,128)(2,1)S(1)} %collective-permute-done.prev), custom_call_target="tpu_custom_call" | custom-call | flops 8589934592 | bytes 4194304 | tf_op jit(solution)/shard_map/cross/pallas_call | solution.py:218
  89.3 0.0 copy-start
  89.3 1.1 copy-done
  90.4 4.4 %all-to-all-start.1 = ((bf16[16,2,2,32,384]{4,3,2,1,0:T(8,128)(2,1)}), bf16[16,2,2,32,384]{4,3,2,1,0:T(8,128)(2,1)S(1)}, u32[]{:S(2)}, u32[]{:S(2)}) async-start(bf16[16,2,2,32,384]{4,3,2,1,0:T(8,128)(2,1)} %copy-done), calls=%async_computation.1 | async-start | bytes 3145728 | tf_op jit(solution)/shard_map/all_to_all | solution.py:280
  94.9 0.1 fusion
  95.0 0.1 reshape.7
  95.1 0.1 copy.7
  95.2 0.1 reshape.8
  95.3 0.1 constant_dynamic-slice_fusion
  95.3 0.1 copy.11.refs_2_
  95.4 0.1 copy.9
  95.5 0.1 slice.19
  95.6 0.1 copy.10.refs_3_
  95.7 20.7 %all-to-all-done.1.refs_0_ = bf16[16,2,2,32,384]{4,3,2,1,0:T(8,128)(2,1)S(1)} async-done(((bf16[16,2,2,32,384]{4,3,2,1,0:T(8,128)(2,1)}), bf16[16,2,2,32,384]{4,3,2,1,0:T(8,128)(2,1)S(1)}, u32[]{:S(2)}, u32[]{:S(2)}) %all-to-all-start.1) | async-done | bytes 1572896 | tf_op jit(solution)/shard_map/all_to_all | solution.py:280
  116.4 0.0 copy-start.2
  116.4 2.2 %copy-done.2 = bf16[1024,2001]{1,0:T(8,128)(2,1)S(1)} copy-done((bf16[1024,2001]{1,0:T(8,128)(2,1)S(1)}, bf16[1024,2001]{1,0:T(8,128)(2,1)}, u32[]{:S(2)}) %copy-start.2) | copy-done | bytes 4098072
  118.6 5.1 %lag_sums.1 = bf16[3,8,32,2001]{3,2,1,0:T(8,128)(2,1)} custom-call(bf16[16,2,2,32,384]{4,3,2,1,0:T(8,128)(2,1)S(1)} %all-to-all-done.1.refs_0_, bf16[1024,2001]{1,0:T(8,128)(2,1)S(1)} %copy-done.2, bf16[8,64]{1,0:T(8,128)(2,1)S(1)} %copy.11.refs_2_, bf16[96,64]{1,0:T(8,128)(2,1)S(1)} %copy.10.refs_3_), custom_call_target="tpu_custom_call" | custom-call | flops 3147300864 | bytes 9437184 | tf_op jit(solution)/shard_map/lag_sums/pallas_call | solution.py:256
  (3 shorter events, 0.0 us)
Async XLA Ops:
  0.8 1.6 %copy-start.1 = (bf16[32,16,2048]{2,1,0:T(8,128)(2,1)S(1)}, bf16[32,16,2048]{2,1,0:T(8,128)(2,1)}, u32[]{:S(2)}) copy-start(bf16[32,16,2048]{2,1,0:T(8,128)(2,1)} %rec.1) | copy-start | bytes 6291460
  36.5 43.4 %collective-permute-start = (bf16[12,264,128]{2,1,0:T(8,128)(2,1)S(1)}, bf16[12,264,128]{2,1,0:T(8,128)(2,1)S(1)}, u32[]{:S(2)}, u32[]{:S(2)}) collective-permute-start(bf16[12,264,128]{2,1,0:T(8,128)(2,1)S(1)} %slice.20), channel_id=1, source_target_pairs={{0,16},{16,32},{32,48},{48,64},{64,80},{80,96},{96,112},{112,128},... | collective-permute-start | bytes 2433032 | tf_op jit(solution)/shard_map/ppermute | solution.py:268
  89.3 1.1 copy-start
  90.4 26.0 %all-to-all-start.1 = ((bf16[16,2,2,32,384]{4,3,2,1,0:T(8,128)(2,1)}), bf16[16,2,2,32,384]{4,3,2,1,0:T(8,128)(2,1)S(1)}, u32[]{:S(2)}, u32[]{:S(2)}) async-start(bf16[16,2,2,32,384]{4,3,2,1,0:T(8,128)(2,1)} %copy-done), calls=%async_computation.1 | async-start | bytes 3145728 | tf_op jit(solution)/shard_map/all_to_all | solution.py:280
  116.4 2.2 %copy-start.2 = (bf16[1024,2001]{1,0:T(8,128)(2,1)S(1)}, bf16[1024,2001]{1,0:T(8,128)(2,1)}, u32[]{:S(2)}) copy-start(bf16[1024,2001]{1,0:T(8,128)(2,1)} %constant.31.clone.refs_1_) | copy-start | bytes 12294148

commit v2 on v1

v2 whole, which is shorter than its diff:
```python
import functools
import math

import jax
import jax.numpy as jnp
import numpy as np
from jax import lax
from jax.experimental import pallas as pl
from jax.experimental.pallas import tpu as pltpu
from jax.sharding import Mesh, PartitionSpec as P

SEG = 2048
NFFT = 4096
BINS = 512
SMOOTH = 4
LAGHALF = 1000
LAGS = 2001
CH = 32
WIN = 16
BF = jnp.bfloat16
F32 = jnp.float32
PARTS = 2
PART_BINS = BINS // PARTS
NB = PART_BINS // 16
PART_ROWS = 8 * NB
STRIDE = NB + 1
LAG_TILE = 1024
LAG_TILES = -(-LAGS // LAG_TILE)
MASK_ROW = PARTS * PART_ROWS
SENT_ROWS = MASK_ROW + 8
OWN_ROWS = SENT_ROWS
NEAR = 16
WIDE = PART_BINS + NEAR
CROSS_FLOPS = (0, 100 << 30)
GROUP = ("x", "zl", "core")
STATIONS = ("y", "zh", "x")


def forward_table(part):
    first = part * (PART_BINS - NEAR)
    phases = np.arange(first + 1, first + WIDE + 1)[:, None] * np.arange(SEG)[None, :] % NFFT
    angles = phases * (2.0 * math.pi / NFFT)
    table = np.concatenate([np.cos(angles), -np.sin(angles)], axis=0) / math.sqrt(SEG)
    return table.astype(np.float32).astype(jnp.bfloat16)


def inverse_table():
    phases = np.arange(1, BINS + 1)[:, None] * (np.arange(LAGS) - LAGHALF)[None, :] % NFFT
    angles = phases * (2.0 * math.pi / NFFT)
    table = np.stack([np.cos(angles), -np.sin(angles)], axis=0) * math.sqrt(2.0 / BINS)
    table = table.reshape(2, PARTS, 16, NB, LAGS).transpose(1, 2, 0, 3, 4)
    table = table.reshape(2 * BINS, LAGS).astype(np.float32).astype(jnp.bfloat16)
    table = np.pad(table, ((0, 0), (0, LAG_TILES * LAG_TILE - LAGS)))
    return table.reshape(2 * BINS, LAG_TILES, LAG_TILE).transpose(1, 0, 2)


def nt_dot(a, b):
    return lax.dot_general(a, b, (((1,), (1,)), ((), ())), preferred_element_type=F32)


def tn_dot(a, b):
    return lax.dot_general(a, b, (((0,), (0,)), ((), ())), preferred_element_type=F32)


def mask_lanes(mask):
    channel = lax.broadcasted_iota(jnp.int32, (CH, 512), 0)
    pick = (lax.broadcasted_iota(jnp.int32, (CH, 512), 1) % CH == channel).astype(BF)
    spread = jnp.dot(mask.astype(F32).astype(BF), pick, preferred_element_type=F32)
    window = lax.broadcasted_iota(jnp.int32, (WIN, 512), 0)
    own_lane = lax.broadcasted_iota(jnp.int32, (WIN, 512), 1) // CH == window
    valid = jnp.sum(jnp.where(own_lane, spread, 0.0), axis=0, keepdims=True)
    return [valid[:, i * 128 : (i + 1) * 128] for i in range(4)]


def whiten(part, rows, table, valid, out, spec, power):
    for ri in range(2):
        value = nt_dot(table[ri * WIDE : (ri + 1) * WIDE, :], rows[...])
        for high in range(4):
            spec[ri, high] = value[:, high * 128 : (high + 1) * 128]
    for high in range(4):
        power[high, 0:8, :] = jnp.zeros((8, 128), F32)
        power[high, 8 + WIDE : 16 + WIDE, :] = jnp.zeros((8, 128), F32)
        real, imag = spec[0, high], spec[1, high]
        power[high, 8 : 8 + WIDE, :] = real * real + imag * imag
    for dst in range(16):
        at = part * NEAR + dst * NB
        bins = part * PART_BINS + dst * NB + lax.broadcasted_iota(jnp.int32, (NB, 128), 0)
        count = jnp.minimum(bins, SMOOTH) + jnp.minimum(BINS - 1 - bins, SMOOTH) + 1
        inverse_count = 1.0 / count.astype(F32)
        for high in range(4):
            total = power[high, 4 + at : 4 + at + NB, :]
            for offset in range(5, 4 + 2 * SMOOTH + 1):
                total = total + power[high, at + offset : at + offset + NB, :]
            factor = valid[high] * lax.rsqrt(total * inverse_count + 0.1)
            for ri in range(2):
                row = part * PART_ROWS + (high * 2 + ri) * NB
                out[dst, row : row + NB, :] = (spec[ri, high, at : at + NB, :] * factor).astype(BF)


def spectra_kernel(rec_far, table_far, mask_far, out, mask, rec, rows, table, planes, spec, power, sems):
    chunk = 4
    copies = [
        pltpu.make_async_copy(rec_far.at[c : c + chunk], rec.at[c : c + chunk], sems.at[c // chunk])
        for c in range(0, CH, chunk)
    ]
    mask_copy = pltpu.make_async_copy(mask_far, mask, sems.at[CH // chunk + PARTS])
    for copy in copies + [mask_copy]:
        copy.start()
    table_copies = [
        pltpu.make_async_copy(table_far.at[part], table.at[part], sems.at[CH // chunk + part])
        for part in range(PARTS)
    ]
    for copy in table_copies:
        copy.start()
    for c in range(0, CH, chunk):
        copies[c // chunk].wait()
        signal = rec[c : c + chunk].astype(F32).reshape(chunk * WIN, SEG)
        centred = signal - jnp.mean(signal, axis=-1, keepdims=True)
        spread = jnp.sqrt(jnp.mean(centred * centred, axis=-1, keepdims=True) + 1e-06)
        normal = centred * (1.0 / spread)
        for t in range(SEG // 128):
            for i in range(chunk):
                planes[t, (c + i) * STRIDE : (c + i) * STRIDE + WIN, :] = normal[i * WIN : (i + 1) * WIN, t * 128 : (t + 1) * 128]
    for w in range(WIN):
        for t in range(SEG // 128):
            rows[w * CH : (w + 1) * CH, t * 128 : (t + 1) * 128] = planes[
                t, pl.ds(w, CH, stride=STRIDE), :
            ].astype(BF)
    mask_copy.wait()
    valid = mask_lanes(mask[...])
    sent_mask = jnp.concatenate(valid + [jnp.zeros((4, 128), F32)], axis=0).astype(BF)
    for dst in range(16):
        out[dst, MASK_ROW:SENT_ROWS, :] = sent_mask
    for part in range(PARTS):
        table_copies[part].wait()
        whiten(part, rows, table.at[part], valid, out, spec, power)


def spectra(records, gap_mask):
    near, far = pl.BlockSpec(memory_space=pltpu.VMEM), pl.BlockSpec(memory_space=pltpu.HBM)
    return pl.pallas_call(
        spectra_kernel,
        out_shape=jax.ShapeDtypeStruct((16, SENT_ROWS, 128), BF),
        in_specs=[far] * 3,
        out_specs=near,
        scratch_shapes=[
            pltpu.VMEM((WIN, CH), jnp.int32),
            pltpu.VMEM((CH, WIN, SEG), BF),
            pltpu.VMEM((512, SEG), BF),
            pltpu.VMEM((PARTS, 2 * WIDE, SEG), BF),
            pltpu.VMEM((SEG // 128, CH * STRIDE, 128), F32),
            pltpu.VMEM((2, 4, WIDE, 128), F32),
            pltpu.VMEM((4, WIDE + 16, 128), F32),
            pltpu.SemaphoreType.DMA((9 + PARTS,)),
        ],
        compiler_params=pltpu.CompilerParams(vmem_limit_bytes=62 << 20),
        cost_estimate=pl.CostEstimate(
            flops=2 * 512 * SEG * 2 * BINS, bytes_accessed=8 << 20, transcendentals=0
        ),
        name="spectra",
    )(records, jnp.asarray(np.stack([forward_table(p) for p in range(PARTS)])), gap_mask.T)


def blocks_to_lanes(parts):
    lane = lax.broadcasted_iota(jnp.int32, parts[0].shape, 1)
    low, odd = lane < 64, (lane // 32) % 2 == 0
    half = []
    a0, a1, a2, a3 = parts
    half = [
        jnp.where(low, a0, pltpu.roll(a2, 64, 1)),
        jnp.where(low, a1, pltpu.roll(a3, 64, 1)),
        jnp.where(low, pltpu.roll(a0, 64, 1), a2),
        jnp.where(low, pltpu.roll(a1, 64, 1), a3),
    ]
    return [
        jnp.where(odd, half[0], pltpu.roll(half[1], 32, 1)),
        jnp.where(odd, pltpu.roll(half[0], 96, 1), half[1]),
        jnp.where(odd, half[2], pltpu.roll(half[3], 32, 1)),
        jnp.where(odd, pltpu.roll(half[2], 96, 1), half[3]),
    ]


def cross_kernel(part, own, prev, out, planes, pairs):
    for block in range(7):
        for v in range(4):
            for ri in range(2):
                source, first = (
                    (prev.at[block * 4 + v], 0)
                    if block < 3
                    else (own.at[(block - 3) * 4 + v], part * PART_ROWS)
                )
                for high in range(4):
                    row = ((block * 2 + ri) * 4 + v) * 4 + high
                    at = first + (high * 2 + ri) * NB
                    planes[row * STRIDE : row * STRIDE + NB, :] = source[at : at + NB, :].astype(F32)
    lane = lax.broadcasted_iota(jnp.int32, (32, 128), 1)

    def one_bin(k, carry):
        def side(blocks):
            found = []
            for ri in range(2):
                parts = [
                    planes[pl.ds((block * 2 + ri) * 16 * STRIDE + k, 16, stride=STRIDE), :] for block in blocks
                ]
                found.append(jnp.concatenate(blocks_to_lanes(parts), axis=0))
            return found

        prev_real, prev_imag = side((0, 0, 1, 2))
        own_real, own_imag = side((3, 4, 5, 6))
        left = jnp.concatenate(
            [
                jnp.concatenate([own_real, own_imag], axis=0),
                jnp.concatenate([own_imag, -own_real], axis=0),
            ],
            axis=1,
        ).astype(BF)
        right = jnp.concatenate(
            [
                jnp.concatenate([prev_real, prev_imag], axis=0),
                jnp.concatenate([own_real, own_imag], axis=0),
            ],
            axis=1,
        ).astype(BF)
        product = tn_dot(left, right)
        for ri in range(2):
            for b in range(4):
                at = ri * 128 + b * 32
                first, second = product[at : at + 32, :128], product[at : at + 32, 128:]
                if b == 3:
                    value = second
                else:
                    value = pltpu.roll(first, 96 - 32 * b, 1)
                    if b:
                        value = jnp.where(lane < 96 - 32 * b, value, pltpu.roll(second, 96 - 32 * b, 1))
                pairs[pl.ds(at * STRIDE + k, 32, stride=STRIDE), :] = value
        return carry

    lax.fori_loop(0, NB, one_bin, 0, unroll=4)
    lanes = lax.broadcasted_iota(jnp.int32, (NB, 128), 1)
    for ri in range(2):
        for b in range(4):
            for v in range(4):
                for high in range(2):
                    row = ri * 128 + b * 32 + v * 8 + high * 4
                    p0, p1, p2, p3 = [pairs[(row + i) * STRIDE : (row + i) * STRIDE + NB, :] for i in range(4)]
                    p1, p2, p3 = pltpu.roll(p1, 96, 1), pltpu.roll(p2, 64, 1), pltpu.roll(p3, 32, 1)
                    target = out.at[b * 4 + v, ri, high]
                    target[:, 0:128] = jnp.where(lanes < 96, p0, p1).astype(BF)
                    target[:, 128:256] = jnp.where(lanes < 64, p1, p2).astype(BF)
                    target[:, 256:384] = jnp.where(lanes < 32, p2, p3).astype(BF)


def cross(part, own, prev):
    full = pl.BlockSpec(memory_space=pltpu.VMEM)
    return pl.pallas_call(
        functools.partial(cross_kernel, part),
        out_shape=jax.ShapeDtypeStruct((16, 2, 2, NB, 384), BF),
        in_specs=[full] * 2,
        out_specs=full,
        scratch_shapes=[
            pltpu.VMEM((7 * 32 * STRIDE, 128), F32),
            pltpu.VMEM((256 * STRIDE, 128), F32),
        ],
        compiler_params=pltpu.CompilerParams(vmem_limit_bytes=48 << 20),
        cost_estimate=pl.CostEstimate(flops=CROSS_FLOPS[part], bytes_accessed=1 << 20, transcendentals=0),
        name="cross",
    )(own, prev)


def turn_kernel(value, out):
    for high in range(2):
        out[high * 384 : (high + 1) * 384, :] = value[:, :, high].reshape(2 * PART_BINS, 384).T


def turn(value):
    near = pl.BlockSpec(memory_space=pltpu.VMEM)
    return pl.pallas_call(
        turn_kernel,
        out_shape=jax.ShapeDtypeStruct((768, 2 * PART_BINS), BF),
        in_specs=[near],
        out_specs=near,
        compiler_params=pltpu.CompilerParams(vmem_limit_bytes=8 << 20),
        cost_estimate=pl.CostEstimate(flops=0, bytes_accessed=4 << 20, transcendentals=0),
        name="turn",
    )(value)


def lag_kernel(first, second, table, own_mask, partner_mask, out, turned, scales):
    @pl.when(pl.program_id(0) == 0)
    def _():
        turned[:, : 2 * PART_BINS] = first[...]
        for high in range(2):
            turned[high * 384 : (high + 1) * 384, 2 * PART_BINS :] = (
                second[:, :, high].reshape(2 * PART_BINS, 384).T
            )
        count = nt_dot(partner_mask[...], own_mask[...])
        scale = 1.0 / jnp.sqrt(jnp.maximum(count, 1.0))
        for c in range(8):
            scales[c * 96 : (c + 1) * 96, :] = jnp.broadcast_to(scale[:, c : c + 1], (96, 128))

    lagged = jnp.dot(turned[...], table[0], preferred_element_type=F32)
    for c in range(8):
        for s in range(3):
            row = c * 96 + s * 32
            for at in range(0, LAG_TILE, 128):
                out[2 - s, c, :, at : at + 128] = (
                    lagged[row : row + 32, at : at + 128] * scales[row : row + 32, :]
                ).astype(BF)


def lag_sums(first, second, own_mask, partner_mask):
    return pl.pallas_call(
        lag_kernel,
        grid=(LAG_TILES,),
        out_shape=jax.ShapeDtypeStruct((3, 8, CH, LAGS), BF),
        in_specs=[
            pl.BlockSpec((768, 2 * PART_BINS), lambda i: (0, 0)),
            pl.BlockSpec((16, 2, 2, NB, 384), lambda i: (0, 0, 0, 0, 0)),
            pl.BlockSpec((1, 2 * BINS, LAG_TILE), lambda i: (i, 0, 0)),
            pl.BlockSpec((8, 64), lambda i: (0, 0)),
            pl.BlockSpec((3 * CH, 64), lambda i: (0, 0)),
        ],
        out_specs=pl.BlockSpec((3, 8, CH, LAG_TILE), lambda i: (0, 0, 0, i)),
        scratch_shapes=[pltpu.VMEM((768, 2 * BINS), BF), pltpu.VMEM((768, 128), F32)],
        compiler_params=pltpu.CompilerParams(vmem_limit_bytes=62 << 20),
        cost_estimate=pl.CostEstimate(
            flops=2 * 768 * 2 * BINS * LAGS, bytes_accessed=9 << 20, transcendentals=0
        ),
        name="lag_sums",
    )(first, second, jnp.asarray(inverse_table()), own_mask, partner_mask)


def shifted(value, axes, count, steps):
    return lax.ppermute(value, axes, [(i, (i + steps) % count) for i in range(count)])


def from_previous_group(value):
    return shifted(value, ("y", "zh"), 16, 1)


def per_device(records, gap_mask):
    own = lax.all_to_all(spectra(records, gap_mask), GROUP, 0, 0, tiled=True)
    prevs = [from_previous_group(own[4:, :PART_ROWS])]
    halo, prevs[0] = lax.optimization_barrier((own[4:, PART_ROWS:], prevs[0]))
    prevs.append(from_previous_group(halo))
    crosses = [
        lax.all_to_all(cross(p, own, prevs[p]), GROUP, 0, 0, tiled=True) for p in range(PARTS)
    ]
    masks = jnp.concatenate([prevs[-1][:, PART_ROWS : PART_ROWS + 4], own[:, MASK_ROW : MASK_ROW + 4]], axis=0)
    masks = lax.dynamic_slice_in_dim(masks, lax.axis_index("x") * 4, 16, 0)
    masks = masks.reshape(4, 16, 4, CH).transpose(0, 3, 1, 2).reshape(4 * CH, 64)
    own_mask = lax.dynamic_slice_in_dim(masks, 3 * CH + lax.axis_index(("zl", "core")) * 8, 8, 0)
    return lag_sums(turn(crosses[0]), crosses[1], own_mask, masks[: 3 * CH])


def solution(mesh):
    fine = Mesh(mesh.devices.reshape(4, 4, 4, 2, 2), ("y", "zh", "x", "zl", "core"))
    in_specs = (P(("y", "zh", "x"), ("zl", "core"), None), P(("y", "zh", "x"), ("zl", "core")))
    out_specs = P(None, ("y", "zh", "x", "zl", "core"), None, None)
    return jax.shard_map(
        per_device, mesh=fine, in_specs=in_specs, out_specs=out_specs, check_vma=False
    )
```

time: 124 us -> 109 us (0.88)
  waiting for transfers between devices: 61.1 us -> 45.9 us
  starting transfers between devices: 7.48 us -> 12.5 us
  local copies, waits for them, and re-layouts: 6.43 us -> 2.83 us
    all_to_all x1 -> x2, waiting for transfers between devices: 20.7 us -> 11.5 us  [per_device(): lax.all_to_all(cross(p, own, prevs[p]), GROUP, 0, 0, tiled=True)]
    ppermute x1 -> x2, waiting for transfers between devices: 40.3 us -> 34.5 us  [shifted(): lax.ppermute(value, axes, [(i, (i + steps) % count) for i in range(count)])]
    all_to_all x1 -> x2, starting transfers between devices: 4.41 us -> 9.44 us  [per_device(): lax.all_to_all(cross(p, own, prevs[p]), GROUP, 0, 0, tiled=True)]
    unnamed x8 -> x3, local copies, waits for them, and re-layouts: 5.76 us -> 1.55 us
    pallas_call x1 -> x2, Pallas kernels: 5.1 us -> 7.42 us  [the longest x1 7.17 us: lag_sums(): pl.pallas_call(lag_kernel, grid=(LAG_TILES,), out_shape=jax.ShapeDtypeStr...]
    pallas_call x1, Pallas kernels: 10.4 us -> 8.2 us  [spectra(): pl.pallas_call(spectra_kernel, out_shape=jax.ShapeDtypeStruct((16, SENT_R...]
    pallas_call x1 -> x2, Pallas kernels: 9.38 us -> 8.09 us  [cross(): pl.pallas_call(functools.partial(cross_kernel, part), out_shape=jax.Shape...]
    ppermute x1 -> x2, starting transfers between devices: 3.06 us -> 3.07 us  [shifted(): lax.ppermute(value, axes, [(i, (i + steps) % count) for i in range(count)])]
  transfers between devices with their start and end apart: 2 -> 4, of which waited for: 2 -> 4; matrix products, arithmetic and copies ran while one was open for 1% -> 2% of each run, Pallas kernels for 0% -> 8%
where the time goes in v2:
time: 109 us
  waiting for transfers between devices  45.9 us (42%)
  blocking collectives  23.9 us (22%)
  Pallas kernels  23.7 us (22%)
  starting transfers between devices  12.5 us (11%)
  local copies, waits for them, and re-layouts  2.83 us (3%)
    ppermute x2, waiting for transfers between devices, shifted(): lax.ppermute(value, axes, [(i, (i + steps) % count) for i in range(count)])  34.5 us
    all_to_all x1, blocking collectives, per_device(): own = lax.all_to_all(spectra(records, gap_mask), GROUP, 0, 0, tiled=True)  23.9 us
    all_to_all x2, waiting for transfers between devices, per_device(): lax.all_to_all(cross(p, own, prevs[p]), GROUP, 0, 0, tiled=True)  11.5 us
    all_to_all x2, starting transfers between devices, per_device(): lax.all_to_all(cross(p, own, prevs[p]), GROUP, 0, 0, tiled=True)  9.44 us
    pallas_call x1, Pallas kernels, spectra(): pl.pallas_call(spectra_kernel, out_shape=jax.ShapeDtypeStruct((16, SENT_R...  8.2 us
    pallas_call x2, Pallas kernels, cross(): pl.pallas_call(functools.partial(cross_kernel, part), out_shape=jax.Shape...  8.09 us
    pallas_call x1, Pallas kernels, lag_sums(): pl.pallas_call(lag_kernel, grid=(LAG_TILES,), out_shape=jax.ShapeDtypeStr...  7.17 us
    ppermute x2, starting transfers between devices, shifted(): lax.ppermute(value, axes, [(i, (i + steps) % count) for i in range(count)])  3.07 us
  transfers between devices with their start and end apart: 4, of which 4 were waited for; matrix products, arithmetic and copies ran while one was open for 2% of the time, Pallas kernels for 8%

profile of v2, /device:TPU:1, one launch (start us, length us, event | category | flops | bytes accessed | tf_op | source)
XLA Modules:
  0.0 109.0 jit_solution(8870909566654060921)
XLA Ops:
  0.0 8.2 %spectra.1 = bf16[16,264,128]{2,1,0:T(8,128)(2,1)} custom-call(bf16[32,16,2048]{2,1,0:T(8,128)(2,1)} %rec_far.1, bf16[2,544,2048]{2,1,0:T(8,128)(2,1)} %constant.30.clone.table_far, s32[16,32]{1,0:T(8,128)} %bitcast.8), custom_call_target="tpu_custom_call" | custom-call | flops 2147483648 | bytes 8388608 | tf_op jit(solution)/shard_map/spectra/pallas_call | solution.py:141
  8.2 23.9 %all_to_all.15.own = bf16[16,264,128]{2,1,0:T(8,128)(2,1)S(1)} all-to-all(bf16[16,264,128]{2,1,0:T(8,128)(2,1)} %spectra.1), channel_id=1, replica_groups=mesh['y'=4,'zh'=4,'x'=4,'zl'=2,'core'=2] {'x','zl','core'}, dimensions={0} | all-to-all | bytes 2162688 | tf_op jit(solution)/shard_map/all_to_all | solution.py:342
  32.1 3.1 %collective-permute-start = (bf16[12,128,128]{2,1,0:T(8,128)(2,1)S(1)}, bf16[12,128,128]{2,1,0:T(8,128)(2,1)S(1)}, u32[]{:S(2)}, u32[]{:S(2)}) collective-permute-start(bf16[12,128,128]{2,1,0:T(8,128)(2,1)S(1)} %slice.25), channel_id=1, source_target_pairs={{0,16},{16,32},{32,48},{48,64},{64,80},{80,96},{96,112},{112,128},... | collective-permute-start | bytes 1179656 | tf_op jit(solution)/shard_map/ppermute | solution.py:334
  35.2 22.3 %collective-permute-done.prev = bf16[12,128,128]{2,1,0:T(8,128)(2,1)S(1)} collective-permute-done((bf16[12,128,128]{2,1,0:T(8,128)(2,1)S(1)}, bf16[12,128,128]{2,1,0:T(8,128)(2,1)S(1)}, u32[]{:S(2)}, u32[]{:S(2)}) %collective-permute-start) | collective-permute-done | bytes 393248 | tf_op jit(solution)/shard_map/ppermute | solution.py:334
  57.5 0.0 collective-permute-start.1
  57.5 4.0 %cross.2 = bf16[16,2,2,16,384]{4,3,2,1,0:T(8,128)(2,1)} custom-call(bf16[16,264,128]{2,1,0:T(8,128)(2,1)S(1)} %all_to_all.15.own, bf16[12,128,128]{2,1,0:T(8,128)(2,1)S(1)} %collective-permute-done.prev), custom_call_target="tpu_custom_call" | custom-call | bytes 1048576 | tf_op jit(solution)/shard_map/cross/pallas_call | solution.py:255
  61.5 4.3 %all-to-all-start.1 = ((bf16[16,2,2,16,384]{4,3,2,1,0:T(8,128)(2,1)}), bf16[16,2,2,16,384]{4,3,2,1,0:T(8,128)(2,1)S(1)}, u32[]{:S(2)}, u32[]{:S(2)}) async-start(bf16[16,2,2,16,384]{4,3,2,1,0:T(8,128)(2,1)} %cross.2), calls=%async_computation.1 | async-start | bytes 1572864 | tf_op jit(solution)/shard_map/all_to_all | solution.py:347
  65.8 12.2 %collective-permute-done.1.prev = bf16[12,136,128]{2,1,0:T(8,128)(2,1)S(1)} collective-permute-done((bf16[12,136,128]{2,1,0:T(8,128)(2,1)S(1)}, bf16[12,136,128]{2,1,0:T(8,128)(2,1)S(1)}, u32[]{:S(2)}, u32[]{:S(2)}) %collective-permute-start.1) | collective-permute-done | bytes 417824 | tf_op jit(solution)/shard_map/ppermute | solution.py:334
  78.0 4.0 %cross.3 = bf16[16,2,2,16,384]{4,3,2,1,0:T(8,128)(2,1)} custom-call(bf16[16,264,128]{2,1,0:T(8,128)(2,1)S(1)} %all_to_all.15.own, bf16[12,136,128]{2,1,0:T(8,128)(2,1)S(1)} %collective-permute-done.1.prev), custom_call_target="tpu_custom_call" | custom-call | flops 107374182400 | bytes 1048576 | tf_op jit(solution)/shard_map/cross/pallas_call | solution.py:255
  82.1 1.5 %all-to-all-done.1.value = bf16[16,2,2,16,384]{4,3,2,1,0:T(8,128)(2,1)S(1)} async-done(((bf16[16,2,2,16,384]{4,3,2,1,0:T(8,128)(2,1)}), bf16[16,2,2,16,384]{4,3,2,1,0:T(8,128)(2,1)S(1)}, u32[]{:S(2)}, u32[]{:S(2)}) %all-to-all-start.1) | async-done | bytes 786464 | tf_op jit(solution)/shard_map/all_to_all | solution.py:347
  83.6 5.1 %all-to-all-start.2 = ((bf16[16,2,2,16,384]{4,3,2,1,0:T(8,128)(2,1)}), bf16[16,2,2,16,384]{4,3,2,1,0:T(8,128)(2,1)}, u32[]{:S(2)}, u32[]{:S(2)}) async-start(bf16[16,2,2,16,384]{4,3,2,1,0:T(8,128)(2,1)} %cross.3), calls=%async_computation.2 | async-start | bytes 1572864 | tf_op jit(solution)/shard_map/all_to_all | solution.py:347
  88.8 0.1 fusion
  88.9 0.1 reshape.7
  89.0 0.1 copy.5
  89.1 0.1 reshape.8
  89.2 0.1 constant_dynamic-slice_fusion
  89.2 0.7 copy.9.own_mask
  90.0 0.1 slice.23
  90.1 0.7 copy.8.partner_mask
  90.8 0.2 turn.1.first
  91.0 0.0 copy-start
  91.1 0.9 copy-done
  91.9 9.9 %all-to-all-done.2.second = bf16[16,2,2,16,384]{4,3,2,1,0:T(8,128)(2,1)} async-done(((bf16[16,2,2,16,384]{4,3,2,1,0:T(8,128)(2,1)}), bf16[16,2,2,16,384]{4,3,2,1,0:T(8,128)(2,1)}, u32[]{:S(2)}, u32[]{:S(2)}) %all-to-all-start.2) | async-done | bytes 786464 | tf_op jit(solution)/shard_map/all_to_all | solution.py:347
  101.8 7.2 %lag_sums.1 = bf16[3,8,32,2001]{3,2,1,0:T(8,128)(2,1)} custom-call(bf16[768,512]{1,0:T(8,128)(2,1)} %copy-done, bf16[16,2,2,16,384]{4,3,2,1,0:T(8,128)(2,1)} %all-to-all-done.2.second, bf16[2,1024,1024]{2,1,0:T(8,128)(2,1)} %constant.31.clone.table, bf16[8,64]{1,0:T(8,128)(2,1)} %copy.9.own_mask, bf16[96,64]{1,0:T(8,128)(2,1)} %copy.8.partner_mask), custom_call_target="tpu_custom_call" | custom-call | flops 3147300864 | bytes 9437184 | tf_op jit(solution)/shard_map/lag_sums/pallas_call | solution.py:312
  (6 shorter events, 0.1 us)
Async XLA Ops:
  32.1 25.4 %collective-permute-start = (bf16[12,128,128]{2,1,0:T(8,128)(2,1)S(1)}, bf16[12,128,128]{2,1,0:T(8,128)(2,1)S(1)}, u32[]{:S(2)}, u32[]{:S(2)}) collective-permute-start(bf16[12,128,128]{2,1,0:T(8,128)(2,1)S(1)} %slice.25), channel_id=1, source_target_pairs={{0,16},{16,32},{32,48},{48,64},{64,80},{80,96},{96,112},{112,128},... | collective-permute-start | bytes 1179656 | tf_op jit(solution)/shard_map/ppermute | solution.py:334
  57.5 20.6 %collective-permute-start.1 = (bf16[12,136,128]{2,1,0:T(8,128)(2,1)S(1)}, bf16[12,136,128]{2,1,0:T(8,128)(2,1)S(1)}, u32[]{:S(2)}, u32[]{:S(2)}) collective-permute-start(bf16[12,136,128]{2,1,0:T(8,128)(2,1)S(1)} %slice.24), channel_id=1, source_target_pairs={{0,16},{16,32},{32,48},{48,64},{64,80},{80,96},{96,112},{112,128},... | collective-permute-start | bytes 1253384 | tf_op jit(solution)/shard_map/ppermute | solution.py:334
  61.5 22.1 %all-to-all-start.1 = ((bf16[16,2,2,16,384]{4,3,2,1,0:T(8,128)(2,1)}), bf16[16,2,2,16,384]{4,3,2,1,0:T(8,128)(2,1)S(1)}, u32[]{:S(2)}, u32[]{:S(2)}) async-start(bf16[16,2,2,16,384]{4,3,2,1,0:T(8,128)(2,1)} %cross.2), calls=%async_computation.1 | async-start | bytes 1572864 | tf_op jit(solution)/shard_map/all_to_all | solution.py:347
  83.6 18.2 %all-to-all-start.2 = ((bf16[16,2,2,16,384]{4,3,2,1,0:T(8,128)(2,1)}), bf16[16,2,2,16,384]{4,3,2,1,0:T(8,128)(2,1)}, u32[]{:S(2)}, u32[]{:S(2)}) async-start(bf16[16,2,2,16,384]{4,3,2,1,0:T(8,128)(2,1)} %cross.3), calls=%async_computation.2 | async-start | bytes 1572864 | tf_op jit(solution)/shard_map/all_to_all | solution.py:347
  91.0 0.9 copy-start

commit v3 on v2

--- a/solution.py
+++ b/solution.py
@@ -24,8 +24,6 @@
 NB = PART_BINS // 16
 PART_ROWS = 8 * NB
 STRIDE = NB + 1
-LAG_TILE = 1024
-LAG_TILES = -(-LAGS // LAG_TILE)
 MASK_ROW = PARTS * PART_ROWS
 SENT_ROWS = MASK_ROW + 8
 OWN_ROWS = SENT_ROWS
@@ -45,13 +43,10 @@
 
 
 def inverse_table():
-    phases = np.arange(1, BINS + 1)[:, None] * (np.arange(LAGS) - LAGHALF)[None, :] % NFFT
+    phases = np.arange(1, BINS + 1)[:, None] * np.arange(LAGHALF, -1, -1)[None, :] % NFFT
     angles = phases * (2.0 * math.pi / NFFT)
     table = np.stack([np.cos(angles), -np.sin(angles)], axis=0) * math.sqrt(2.0 / BINS)
-    table = table.reshape(2, PARTS, 16, NB, LAGS).transpose(1, 2, 0, 3, 4)
-    table = table.reshape(2 * BINS, LAGS).astype(np.float32).astype(jnp.bfloat16)
-    table = np.pad(table, ((0, 0), (0, LAG_TILES * LAG_TILE - LAGS)))
-    return table.reshape(2 * BINS, LAG_TILES, LAG_TILE).transpose(1, 0, 2)
+    return np.pad(table, ((0, 0), (0, 0), (0, 23))).astype(np.float32).astype(jnp.bfloat16)
 
 
 def nt_dot(a, b):
@@ -148,7 +143,7 @@
             pltpu.VMEM((CH, WIN, SEG), BF),
             pltpu.VMEM((512, SEG), BF),
             pltpu.VMEM((PARTS, 2 * WIDE, SEG), BF),
-            pltpu.VMEM((SEG // 128, CH * STRIDE, 128), F32),
+            pltpu.VMEM((SEG // 128, CH * STRIDE + 32, 128), F32),
             pltpu.VMEM((2, 4, WIDE, 128), F32),
             pltpu.VMEM((4, WIDE + 16, 128), F32),
             pltpu.SemaphoreType.DMA((9 + PARTS,)),
@@ -161,26 +156,22 @@
     )(records, jnp.asarray(np.stack([forward_table(p) for p in range(PARTS)])), gap_mask.T)
 
 
+def rolled(value, lanes):
+    return pltpu.roll(value, lanes % 128, 1) if lanes % 128 else value
+
+
 def blocks_to_lanes(parts):
-    lane = lax.broadcasted_iota(jnp.int32, parts[0].shape, 1)
-    low, odd = lane < 64, (lane // 32) % 2 == 0
-    half = []
-    a0, a1, a2, a3 = parts
-    half = [
-        jnp.where(low, a0, pltpu.roll(a2, 64, 1)),
-        jnp.where(low, a1, pltpu.roll(a3, 64, 1)),
-        jnp.where(low, pltpu.roll(a0, 64, 1), a2),
-        jnp.where(low, pltpu.roll(a1, 64, 1), a3),
-    ]
-    return [
-        jnp.where(odd, half[0], pltpu.roll(half[1], 32, 1)),
-        jnp.where(odd, pltpu.roll(half[0], 96, 1), half[1]),
-        jnp.where(odd, half[2], pltpu.roll(half[3], 32, 1)),
-        jnp.where(odd, pltpu.roll(half[2], 96, 1), half[3]),
-    ]
-
-
-def cross_kernel(part, own, prev, out, planes, pairs):
+    slot = lax.broadcasted_iota(jnp.int32, parts[0].shape, 1) // 32
+    found = []
+    for low in range(4):
+        value = parts[-low % 4]
+        for at in range(1, 4):
+            value = jnp.where(slot == at, parts[(at - low) % 4], value)
+        found.append(rolled(value, -32 * low))
+    return found
+
+
+def cross_kernel(part, own, prev, out_far, planes, pairs, out, sems):
     for block in range(7):
         for v in range(4):
             for ri in range(2):
@@ -192,7 +183,8 @@
                 for high in range(4):
                     row = ((block * 2 + ri) * 4 + v) * 4 + high
                     at = first + (high * 2 + ri) * NB
-                    planes[row * STRIDE : row * STRIDE + NB, :] = source[at : at + NB, :].astype(F32)
+                    value = source[at : at + NB, :].astype(F32)
+                    planes[row * STRIDE : row * STRIDE + NB, :] = rolled(value, 32 * (block + 1 if block < 3 else block - 3))
     lane = lax.broadcasted_iota(jnp.int32, (32, 128), 1)
 
     def one_bin(k, carry):
@@ -226,28 +218,31 @@
             for b in range(4):
                 at = ri * 128 + b * 32
                 first, second = product[at : at + 32, :128], product[at : at + 32, 128:]
-                if b == 3:
-                    value = second
-                else:
-                    value = pltpu.roll(first, 96 - 32 * b, 1)
-                    if b:
-                        value = jnp.where(lane < 96 - 32 * b, value, pltpu.roll(second, 96 - 32 * b, 1))
+                value = jnp.where(lane < 32 * b + 32, second, first)
                 pairs[pl.ds(at * STRIDE + k, 32, stride=STRIDE), :] = value
         return carry
 
-    lax.fori_loop(0, NB, one_bin, 0, unroll=4)
+    lax.fori_loop(0, NB, one_bin, 0, unroll=8)
     lanes = lax.broadcasted_iota(jnp.int32, (NB, 128), 1)
-    for ri in range(2):
-        for b in range(4):
+    copies = []
+    for b in range(4):
+        for ri in range(2):
             for v in range(4):
                 for high in range(2):
                     row = ri * 128 + b * 32 + v * 8 + high * 4
                     p0, p1, p2, p3 = [pairs[(row + i) * STRIDE : (row + i) * STRIDE + NB, :] for i in range(4)]
-                    p1, p2, p3 = pltpu.roll(p1, 96, 1), pltpu.roll(p2, 64, 1), pltpu.roll(p3, 32, 1)
+                    first = 32 * b + 32
+                    p0, p1 = rolled(p0, -first), rolled(p1, 96 - first)
+                    p2, p3 = rolled(p2, 64 - first), rolled(p3, 32 - first)
                     target = out.at[b * 4 + v, ri, high]
                     target[:, 0:128] = jnp.where(lanes < 96, p0, p1).astype(BF)
                     target[:, 128:256] = jnp.where(lanes < 64, p1, p2).astype(BF)
                     target[:, 256:384] = jnp.where(lanes < 32, p2, p3).astype(BF)
+        dsts = pl.ds(b * 4, 4)
+        copies.append(pltpu.make_async_copy(out.at[dsts], out_far.at[dsts], sems.at[b]))
+        copies[b].start()
+    for copy in copies:
+        copy.wait()
 
 
 def cross(part, own, prev):
@@ -256,10 +251,12 @@
         functools.partial(cross_kernel, part),
         out_shape=jax.ShapeDtypeStruct((16, 2, 2, NB, 384), BF),
         in_specs=[full] * 2,
-        out_specs=full,
+        out_specs=pl.BlockSpec(memory_space=pltpu.HBM),
         scratch_shapes=[
-            pltpu.VMEM((7 * 32 * STRIDE, 128), F32),
-            pltpu.VMEM((256 * STRIDE, 128), F32),
+            pltpu.VMEM((7 * 32 * STRIDE + 32, 128), F32),
+            pltpu.VMEM((256 * STRIDE + 32, 128), F32),
+            pltpu.VMEM((16, 2, 2, NB, 384), BF),
+            pltpu.SemaphoreType.DMA((4,)),
         ],
         compiler_params=pltpu.CompilerParams(vmem_limit_bytes=48 << 20),
         cost_estimate=pl.CostEstimate(flops=CROSS_FLOPS[part], bytes_accessed=1 << 20, transcendentals=0),
@@ -267,67 +264,103 @@
     )(own, prev)
 
 
-def turn_kernel(value, out):
-    for high in range(2):
-        out[high * 384 : (high + 1) * 384, :] = value[:, :, high].reshape(2 * PART_BINS, 384).T
-
-
-def turn(value):
+def turned(value, ri, high):
+    return value[:, ri, high].reshape(PART_BINS, 384).T
+
+
+def turn_kernel(value, own_mask, partner_mask, table_far, out, scales, table, sem):
+    copy = pltpu.make_async_copy(table_far, table, sem)
+    copy.start()
+    for ri in range(2):
+        for high in range(2):
+            out[ri, high * 384 : (high + 1) * 384, :] = turned(value, ri, high)
+    count = nt_dot(partner_mask[...], own_mask[...])
+    scale = 1.0 / jnp.sqrt(jnp.maximum(count, 1.0))
+    for c in range(8):
+        scales[c * 96 : (c + 1) * 96, :] = jnp.broadcast_to(scale[:, c : c + 1], (96, 128))
+    copy.wait()
+
+
+def turn(value, own_mask, partner_mask):
     near = pl.BlockSpec(memory_space=pltpu.VMEM)
     return pl.pallas_call(
         turn_kernel,
-        out_shape=jax.ShapeDtypeStruct((768, 2 * PART_BINS), BF),
-        in_specs=[near],
-        out_specs=near,
+        out_shape=[
+            jax.ShapeDtypeStruct((2, 768, PART_BINS), BF),
+            jax.ShapeDtypeStruct((768, 128), F32),
+            jax.ShapeDtypeStruct((BINS, 1024), BF),
+        ],
+        in_specs=[near] * 3 + [pl.BlockSpec(memory_space=pltpu.HBM)],
+        out_specs=[near] * 3,
+        scratch_shapes=[pltpu.SemaphoreType.DMA],
         compiler_params=pltpu.CompilerParams(vmem_limit_bytes=8 << 20),
         cost_estimate=pl.CostEstimate(flops=0, bytes_accessed=4 << 20, transcendentals=0),
         name="turn",
-    )(value)
-
-
-def lag_kernel(first, second, table, own_mask, partner_mask, out, turned, scales):
-    @pl.when(pl.program_id(0) == 0)
-    def _():
-        turned[:, : 2 * PART_BINS] = first[...]
-        for high in range(2):
-            turned[high * 384 : (high + 1) * 384, 2 * PART_BINS :] = (
-                second[:, :, high].reshape(2 * PART_BINS, 384).T
+    )(value, own_mask, partner_mask, jnp.asarray(inverse_table()[0]))
+
+
+def lag_kernel(first, second, scales, cosines, sines, out, left, back):
+    for ri in range(2):
+        left[ri, :, :PART_BINS] = first[ri]
+        left[ri, :, PART_BINS:] = turned(second, ri, 0)
+    row = lax.broadcasted_iota(jnp.int32, (256, 256), 0)
+    col = lax.broadcasted_iota(jnp.int32, (256, 256), 1)
+    reverse = ((row // 128 == col // 128) & ((row + col) % 128 == 80)).astype(BF)
+    lane = lax.broadcasted_iota(jnp.int32, (CH, 128), 1)
+    for at in (512, 0):
+        even = jnp.dot(left[0], cosines[:, at : at + 512], preferred_element_type=F32)
+        odd = jnp.dot(left[1], sines[:, at : at + 512], preferred_element_type=F32)
+        ahead, behind = even + odd, even - odd
+        for pair in range(2):
+            both = []
+            for tile in range(2):
+                lanes = slice((pair * 2 + tile) * 128, (pair * 2 + tile + 1) * 128)
+                both.append((ahead[:, lanes] * scales[...]).astype(BF))
+            back[:, at + pair * 256 : at + pair * 256 + 256] = jnp.dot(
+                jnp.concatenate(both, axis=1), reverse, preferred_element_type=F32
             )
-        count = nt_dot(partner_mask[...], own_mask[...])
-        scale = 1.0 / jnp.sqrt(jnp.maximum(count, 1.0))
-        for c in range(8):
-            scales[c * 96 : (c + 1) * 96, :] = jnp.broadcast_to(scale[:, c : c + 1], (96, 128))
-
-    lagged = jnp.dot(turned[...], table[0], preferred_element_type=F32)
-    for c in range(8):
+        for low in range(4):
+            for s in range(3):
+                rows = slice(low * 96 + s * 32, low * 96 + s * 32 + 32)
+                for tile in range(4):
+                    lanes = slice(tile * 128, (tile + 1) * 128)
+                    value = behind[rows, lanes] * scales[rows, :]
+                    if at + tile * 128 == 896:
+                        value = jnp.where(lane <= LAGHALF - 896, value, back[rows, 896:1024])
+                    out[2 - s, low, :, at + tile * 128 : at + (tile + 1) * 128] = value.astype(BF)
+    for low in range(4):
         for s in range(3):
-            row = c * 96 + s * 32
-            for at in range(0, LAG_TILE, 128):
-                out[2 - s, c, :, at : at + 128] = (
-                    lagged[row : row + 32, at : at + 128] * scales[row : row + 32, :]
-                ).astype(BF)
-
-
-def lag_sums(first, second, own_mask, partner_mask):
+            rows = slice(low * 96 + s * 32, low * 96 + s * 32 + 32)
+            for tile in range(8):
+                high_lanes = back[rows, (7 - tile) * 128 : (8 - tile) * 128]
+                if tile < 7:
+                    low_lanes = back[rows, (6 - tile) * 128 : (7 - tile) * 128]
+                    value = jnp.where(lane <= 80, high_lanes, low_lanes)
+                    out[2 - s, low, :, 1024 + tile * 128 : 1152 + tile * 128] = value.astype(BF)
+                else:
+                    out[2 - s, low, :, 1920:LAGS] = high_lanes[:, : LAGS - 1920].astype(BF)
+
+
+def lag_sums(first, second, scales, cosines):
     return pl.pallas_call(
         lag_kernel,
-        grid=(LAG_TILES,),
+        grid=(2,),
         out_shape=jax.ShapeDtypeStruct((3, 8, CH, LAGS), BF),
         in_specs=[
-            pl.BlockSpec((768, 2 * PART_BINS), lambda i: (0, 0)),
-            pl.BlockSpec((16, 2, 2, NB, 384), lambda i: (0, 0, 0, 0, 0)),
-            pl.BlockSpec((1, 2 * BINS, LAG_TILE), lambda i: (i, 0, 0)),
-            pl.BlockSpec((8, 64), lambda i: (0, 0)),
-            pl.BlockSpec((3 * CH, 64), lambda i: (0, 0)),
+            pl.BlockSpec((2, 384, PART_BINS), lambda h: (0, h, 0)),
+            pl.BlockSpec((16, 2, 1, NB, 384), lambda h: (0, 0, h, 0, 0)),
+            pl.BlockSpec((384, 128), lambda h: (h, 0)),
+            pl.BlockSpec((BINS, 1024), lambda h: (0, 0)),
+            pl.BlockSpec((BINS, 1024), lambda h: (0, 0)),
         ],
-        out_specs=pl.BlockSpec((3, 8, CH, LAG_TILE), lambda i: (0, 0, 0, i)),
-        scratch_shapes=[pltpu.VMEM((768, 2 * BINS), BF), pltpu.VMEM((768, 128), F32)],
-        compiler_params=pltpu.CompilerParams(vmem_limit_bytes=62 << 20),
+        out_specs=pl.BlockSpec((3, 4, CH, LAGS), lambda h: (0, h, 0, 0)),
+        scratch_shapes=[pltpu.VMEM((2, 384, BINS), BF), pltpu.VMEM((384, 1024), F32)],
+        compiler_params=pltpu.CompilerParams(vmem_limit_bytes=59 << 20),
         cost_estimate=pl.CostEstimate(
-            flops=2 * 768 * 2 * BINS * LAGS, bytes_accessed=9 << 20, transcendentals=0
+            flops=768 * 2 * BINS * LAGS, bytes_accessed=7 << 20, transcendentals=0
         ),
         name="lag_sums",
-    )(first, second, jnp.asarray(inverse_table()), own_mask, partner_mask)
+    )(first, second, scales, cosines, jnp.asarray(inverse_table()[1]))
 
 
 def shifted(value, axes, count, steps):
@@ -350,7 +383,8 @@
     masks = lax.dynamic_slice_in_dim(masks, lax.axis_index("x") * 4, 16, 0)
     masks = masks.reshape(4, 16, 4, CH).transpose(0, 3, 1, 2).reshape(4 * CH, 64)
     own_mask = lax.dynamic_slice_in_dim(masks, 3 * CH + lax.axis_index(("zl", "core")) * 8, 8, 0)
-    return lag_sums(turn(crosses[0]), crosses[1], own_mask, masks[: 3 * CH])
+    first, scales, cosines = turn(crosses[0], own_mask, masks[: 3 * CH])
+    return lag_sums(first, crosses[1], scales, cosines)
 
 
 def solution(mesh):

time: 109 us -> 108 us (level)
  Pallas kernels: 23.7 us -> 20.4 us
  local copies, waits for them, and re-layouts: 2.83 us -> 4.25 us
    pallas_call x2, Pallas kernels: 8.09 us -> 5.93 us  [cross(): pl.pallas_call(functools.partial(cross_kernel, part), out_shape=jax.Shape...]
    unnamed x3 -> x11, local copies, waits for them, and re-layouts: 1.55 us -> 3.58 us
    ppermute x2, waiting for transfers between devices: 34.5 us -> 35.8 us  [shifted(): lax.ppermute(value, axes, [(i, (i + steps) % count) for i in range(count)])]
    pallas_call x2, Pallas kernels: 7.42 us -> 6.23 us  [the longest x1 5.76 us: lag_sums(): pl.pallas_call(lag_kernel, grid=(2,), out_shape=jax.ShapeDtypeStruct((3,...]
  transfers between devices with their start and end apart: 4 -> 4, of which waited for: 4 -> 4; matrix products, arithmetic and copies ran while one was open for 2% -> 1% of each run, Pallas kernels for 8% -> 6%
where the time goes in v3:
time: 108 us
  waiting for transfers between devices  46.4 us (43%)
  blocking collectives  23.8 us (22%)
  Pallas kernels  20.4 us (19%)
  starting transfers between devices  12.5 us (12%)
  local copies, waits for them, and re-layouts  4.25 us (4%)
    ppermute x2, waiting for transfers between devices, shifted(): lax.ppermute(value, axes, [(i, (i + steps) % count) for i in range(count)])  35.8 us
    all_to_all x1, blocking collectives, per_device(): own = lax.all_to_all(spectra(records, gap_mask), GROUP, 0, 0, tiled=True)  23.8 us
    all_to_all x2, waiting for transfers between devices, per_device(): lax.all_to_all(cross(p, own, prevs[p]), GROUP, 0, 0, tiled=True)  10.7 us
    all_to_all x2, starting transfers between devices, per_device(): lax.all_to_all(cross(p, own, prevs[p]), GROUP, 0, 0, tiled=True)  9.45 us
    pallas_call x1, Pallas kernels, spectra(): pl.pallas_call(spectra_kernel, out_shape=jax.ShapeDtypeStruct((16, SENT_R...  8.2 us
    pallas_call x2, Pallas kernels, cross(): pl.pallas_call(functools.partial(cross_kernel, part), out_shape=jax.Shape...  5.93 us
    pallas_call x1, Pallas kernels, lag_sums(): pl.pallas_call(lag_kernel, grid=(2,), out_shape=jax.ShapeDtypeStruct((3,...  5.76 us
    unnamed x11, local copies, waits for them, and re-layouts  3.58 us
  transfers between devices with their start and end apart: 4, of which 4 were waited for; matrix products, arithmetic and copies ran while one was open for 1% of the time, Pallas kernels for 6%

profile of v3, /device:TPU:1, one launch (start us, length us, event | category | flops | bytes accessed | tf_op | source)
XLA Modules:
  0.0 107.6 jit_solution(5992393695892006523)
XLA Ops:
  0.0 8.2 %spectra.1 = bf16[16,264,128]{2,1,0:T(8,128)(2,1)} custom-call(bf16[32,16,2048]{2,1,0:T(8,128)(2,1)} %rec_far.1, bf16[2,544,2048]{2,1,0:T(8,128)(2,1)} %constant.32.clone.table_far, s32[16,32]{1,0:T(8,128)} %bitcast.8), custom_call_target="tpu_custom_call" | custom-call | flops 2147483648 | bytes 8388608 | tf_op jit(solution)/shard_map/spectra/pallas_call | solution.py:136
  8.2 23.8 %all_to_all.15.own = bf16[16,264,128]{2,1,0:T(8,128)(2,1)S(1)} all-to-all(bf16[16,264,128]{2,1,0:T(8,128)(2,1)} %spectra.1), channel_id=1, replica_groups=mesh['y'=4,'zh'=4,'x'=4,'zl'=2,'core'=2] {'x','zl','core'}, dimensions={0} | all-to-all | bytes 2162688 | tf_op jit(solution)/shard_map/all_to_all | solution.py:375
  32.1 3.1 %collective-permute-start = (bf16[12,128,128]{2,1,0:T(8,128)(2,1)S(1)}, bf16[12,128,128]{2,1,0:T(8,128)(2,1)S(1)}, u32[]{:S(2)}, u32[]{:S(2)}) collective-permute-start(bf16[12,128,128]{2,1,0:T(8,128)(2,1)S(1)} %slice.25), channel_id=1, source_target_pairs={{0,16},{16,32},{32,48},{48,64},{64,80},{80,96},{96,112},{112,128},... | collective-permute-start | bytes 1179656 | tf_op jit(solution)/shard_map/ppermute | solution.py:367
  35.2 22.3 %collective-permute-done.prev = bf16[12,128,128]{2,1,0:T(8,128)(2,1)S(1)} collective-permute-done((bf16[12,128,128]{2,1,0:T(8,128)(2,1)S(1)}, bf16[12,128,128]{2,1,0:T(8,128)(2,1)S(1)}, u32[]{:S(2)}, u32[]{:S(2)}) %collective-permute-start) | collective-permute-done | bytes 393248 | tf_op jit(solution)/shard_map/ppermute | solution.py:367
  57.5 0.0 collective-permute-start.1
  57.5 2.7 %cross.2 = bf16[16,2,2,16,384]{4,3,2,1,0:T(8,128)(2,1)} custom-call(bf16[16,264,128]{2,1,0:T(8,128)(2,1)S(1)} %all_to_all.15.own, bf16[12,128,128]{2,1,0:T(8,128)(2,1)S(1)} %collective-permute-done.prev), custom_call_target="tpu_custom_call" | custom-call | bytes 1048576 | tf_op jit(solution)/shard_map/cross/pallas_call | solution.py:250
  60.2 4.3 %all-to-all-start.1 = ((bf16[16,2,2,16,384]{4,3,2,1,0:T(8,128)(2,1)}), bf16[16,2,2,16,384]{4,3,2,1,0:T(8,128)(2,1)S(1)}, u32[]{:S(2)}, u32[]{:S(2)}) async-start(bf16[16,2,2,16,384]{4,3,2,1,0:T(8,128)(2,1)} %cross.2), calls=%async_computation.1 | async-start | bytes 1572864 | tf_op jit(solution)/shard_map/all_to_all | solution.py:380
  64.5 13.5 %collective-permute-done.1.prev = bf16[12,136,128]{2,1,0:T(8,128)(2,1)S(1)} collective-permute-done((bf16[12,136,128]{2,1,0:T(8,128)(2,1)S(1)}, bf16[12,136,128]{2,1,0:T(8,128)(2,1)S(1)}, u32[]{:S(2)}, u32[]{:S(2)}) %collective-permute-start.1) | collective-permute-done | bytes 417824 | tf_op jit(solution)/shard_map/ppermute | solution.py:367
  78.0 3.2 %cross.3 = bf16[16,2,2,16,384]{4,3,2,1,0:T(8,128)(2,1)S(1)} custom-call(bf16[16,264,128]{2,1,0:T(8,128)(2,1)S(1)} %all_to_all.15.own, bf16[12,136,128]{2,1,0:T(8,128)(2,1)S(1)} %collective-permute-done.1.prev), custom_call_target="tpu_custom_call" | custom-call | flops 107374182400 | bytes 1048576 | tf_op jit(solution)/shard_map/cross/pallas_call | solution.py:250
  81.2 0.0 copy-start.3
  81.3 0.9 copy-done.3
  82.2 0.0 copy-start.1
  82.2 1.5 %all-to-all-done.1.value = bf16[16,2,2,16,384]{4,3,2,1,0:T(8,128)(2,1)S(1)} async-done(((bf16[16,2,2,16,384]{4,3,2,1,0:T(8,128)(2,1)}), bf16[16,2,2,16,384]{4,3,2,1,0:T(8,128)(2,1)S(1)}, u32[]{:S(2)}, u32[]{:S(2)}) %all-to-all-start.1) | async-done | bytes 786464 | tf_op jit(solution)/shard_map/all_to_all | solution.py:380
  83.7 5.1 %all-to-all-start.2 = ((bf16[16,2,2,16,384]{4,3,2,1,0:T(8,128)(2,1)}), bf16[16,2,2,16,384]{4,3,2,1,0:T(8,128)(2,1)}, u32[]{:S(2)}, u32[]{:S(2)}) async-start(bf16[16,2,2,16,384]{4,3,2,1,0:T(8,128)(2,1)} %copy-done.3), calls=%async_computation.2 | async-start | bytes 1572864 | tf_op jit(solution)/shard_map/all_to_all | solution.py:380
  88.8 0.1 fusion
  88.9 0.1 reshape.7
  89.0 0.1 copy.6
  89.1 0.1 reshape.8
  89.2 0.1 constant_dynamic-slice_fusion
  89.3 0.1 copy.10.own_mask
  89.4 0.1 copy.8
  89.4 0.1 slice.23
  89.5 0.1 copy.9.partner_mask
  89.6 0.0 copy-done.1
  89.6 0.5 turn.1
  90.1 0.0 copy-start
  90.1 1.0 copy-done
  91.1 0.0 copy-start.2
  91.1 0.9 copy-done.2
  92.0 0.0 copy-start.4
  92.0 0.7 copy-done.4
  92.7 9.2 %all-to-all-done.2.second = bf16[16,2,2,16,384]{4,3,2,1,0:T(8,128)(2,1)} async-done(((bf16[16,2,2,16,384]{4,3,2,1,0:T(8,128)(2,1)}), bf16[16,2,2,16,384]{4,3,2,1,0:T(8,128)(2,1)}, u32[]{:S(2)}, u32[]{:S(2)}) %all-to-all-start.2) | async-done | bytes 786464 | tf_op jit(solution)/shard_map/all_to_all | solution.py:380
  101.9 5.8 %lag_sums.1 = bf16[3,8,32,2001]{3,2,1,0:T(8,128)(2,1)} custom-call(bf16[2,768,256]{2,1,0:T(8,128)(2,1)} %copy-done.2, bf16[16,2,2,16,384]{4,3,2,1,0:T(8,128)(2,1)} %all-to-all-done.2.second, f32[768,128]{1,0:T(8,128)} %copy-done.4, bf16[512,1024]{1,0:T(8,128)(2,1)} %copy-done, bf16[512,1024]{1,0:T(8,128)(2,1)} %constant.34.clone.sines), custom_call_target="tpu_custom_call" | custom-call | flops 1573650432 | bytes 7340032 | tf_op jit(solution)/shard_map/lag_sums/pallas_call | solution.py:345
  (5 shorter events, 0.1 us)
Async XLA Ops:
  32.1 25.4 %collective-permute-start = (bf16[12,128,128]{2,1,0:T(8,128)(2,1)S(1)}, bf16[12,128,128]{2,1,0:T(8,128)(2,1)S(1)}, u32[]{:S(2)}, u32[]{:S(2)}) collective-permute-start(bf16[12,128,128]{2,1,0:T(8,128)(2,1)S(1)} %slice.25), channel_id=1, source_target_pairs={{0,16},{16,32},{32,48},{48,64},{64,80},{80,96},{96,112},{112,128},... | collective-permute-start | bytes 1179656 | tf_op jit(solution)/shard_map/ppermute | solution.py:367
  57.5 20.6 %collective-permute-start.1 = (bf16[12,136,128]{2,1,0:T(8,128)(2,1)S(1)}, bf16[12,136,128]{2,1,0:T(8,128)(2,1)S(1)}, u32[]{:S(2)}, u32[]{:S(2)}) collective-permute-start(bf16[12,136,128]{2,1,0:T(8,128)(2,1)S(1)} %slice.24), channel_id=1, source_target_pairs={{0,16},{16,32},{32,48},{48,64},{64,80},{80,96},{96,112},{112,128},... | collective-permute-start | bytes 1253384 | tf_op jit(solution)/shard_map/ppermute | solution.py:367
  60.2 23.5 %all-to-all-start.1 = ((bf16[16,2,2,16,384]{4,3,2,1,0:T(8,128)(2,1)}), bf16[16,2,2,16,384]{4,3,2,1,0:T(8,128)(2,1)S(1)}, u32[]{:S(2)}, u32[]{:S(2)}) async-start(bf16[16,2,2,16,384]{4,3,2,1,0:T(8,128)(2,1)} %cross.2), calls=%async_computation.1 | async-start | bytes 1572864 | tf_op jit(solution)/shard_map/all_to_all | solution.py:380
  81.2 0.9 copy-start.3
  82.2 7.5 %copy-start.1 = (bf16[512,1024]{1,0:T(8,128)(2,1)S(1)}, bf16[512,1024]{1,0:T(8,128)(2,1)}, u32[]{:S(2)}) copy-start(bf16[512,1024]{1,0:T(8,128)(2,1)} %constant.33.clone.table_far) | copy-start | bytes 3145732
  83.7 18.2 %all-to-all-start.2 = ((bf16[16,2,2,16,384]{4,3,2,1,0:T(8,128)(2,1)}), bf16[16,2,2,16,384]{4,3,2,1,0:T(8,128)(2,1)}, u32[]{:S(2)}, u32[]{:S(2)}) async-start(bf16[16,2,2,16,384]{4,3,2,1,0:T(8,128)(2,1)} %copy-done.3), calls=%async_computation.2 | async-start | bytes 1572864 | tf_op jit(solution)/shard_map/all_to_all | solution.py:380
  90.1 1.0 copy-start
  91.1 0.9 copy-start.2
  92.0 0.7 copy-start.4

commit v4 on v3

--- a/solution.py
+++ b/solution.py
@@ -67,7 +67,7 @@
     return [valid[:, i * 128 : (i + 1) * 128] for i in range(4)]
 
 
-def whiten(part, rows, table, valid, out, spec, power):
+def multiply(rows, table, spec, power):
     for ri in range(2):
         value = nt_dot(table[ri * WIDE : (ri + 1) * WIDE, :], rows[...])
         for high in range(4):
@@ -77,22 +77,24 @@
         power[high, 8 + WIDE : 16 + WIDE, :] = jnp.zeros((8, 128), F32)
         real, imag = spec[0, high], spec[1, high]
         power[high, 8 : 8 + WIDE, :] = real * real + imag * imag
-    for dst in range(16):
-        at = part * NEAR + dst * NB
-        bins = part * PART_BINS + dst * NB + lax.broadcasted_iota(jnp.int32, (NB, 128), 0)
-        count = jnp.minimum(bins, SMOOTH) + jnp.minimum(BINS - 1 - bins, SMOOTH) + 1
-        inverse_count = 1.0 / count.astype(F32)
-        for high in range(4):
-            total = power[high, 4 + at : 4 + at + NB, :]
-            for offset in range(5, 4 + 2 * SMOOTH + 1):
-                total = total + power[high, at + offset : at + offset + NB, :]
-            factor = valid[high] * lax.rsqrt(total * inverse_count + 0.1)
-            for ri in range(2):
-                row = part * PART_ROWS + (high * 2 + ri) * NB
-                out[dst, row : row + NB, :] = (spec[ri, high, at : at + NB, :] * factor).astype(BF)
-
-
-def spectra_kernel(rec_far, table_far, mask_far, out, mask, rec, rows, table, planes, spec, power, sems):
+
+
+def whiten(part, dst, valid, out, spec, power):
+    at = part * NEAR + dst * NB
+    bins = part * PART_BINS + dst * NB + lax.broadcasted_iota(jnp.int32, (NB, 128), 0)
+    count = jnp.minimum(bins, SMOOTH) + jnp.minimum(BINS - 1 - bins, SMOOTH) + 1
+    inverse_count = 1.0 / count.astype(F32)
+    for high in range(4):
+        total = power[high, 4 + at : 4 + at + NB, :]
+        for offset in range(5, 4 + 2 * SMOOTH + 1):
+            total = total + power[high, at + offset : at + offset + NB, :]
+        factor = valid[high] * lax.rsqrt(total * inverse_count + 0.1)
+        for ri in range(2):
+            row = part * PART_ROWS + (high * 2 + ri) * NB
+            out[dst, row : row + NB, :] = (spec[ri, high, at : at + NB, :] * factor).astype(BF)
+
+
+def spectra_kernel(rec_far, table_far, mask_far, out_far, out, mask, rec, rows, table, planes, spec, power, sems, out_sems):
     chunk = 4
     copies = [
         pltpu.make_async_copy(rec_far.at[c : c + chunk], rec.at[c : c + chunk], sems.at[c // chunk])
@@ -124,29 +126,42 @@
     mask_copy.wait()
     valid = mask_lanes(mask[...])
     sent_mask = jnp.concatenate(valid + [jnp.zeros((4, 128), F32)], axis=0).astype(BF)
-    for dst in range(16):
-        out[dst, MASK_ROW:SENT_ROWS, :] = sent_mask
     for part in range(PARTS):
         table_copies[part].wait()
-        whiten(part, rows, table.at[part], valid, out, spec, power)
+        multiply(rows, table.at[part], spec.at[part], power.at[part])
+    out_copies = []
+    for first in range(0, 16, 4):
+        for dst in range(first, first + 4):
+            for part in range(PARTS):
+                whiten(part, dst, valid, out, spec.at[part], power.at[part])
+            out[dst, MASK_ROW:SENT_ROWS, :] = sent_mask
+        dsts = pl.ds(first, 4)
+        out_copies.append(
+            pltpu.make_async_copy(out.at[dsts], out_far.at[dsts], out_sems.at[first // 4])
+        )
+        out_copies[-1].start()
+    for copy in out_copies:
+        copy.wait()
 
 
 def spectra(records, gap_mask):
-    near, far = pl.BlockSpec(memory_space=pltpu.VMEM), pl.BlockSpec(memory_space=pltpu.HBM)
+    far = pl.BlockSpec(memory_space=pltpu.HBM)
     return pl.pallas_call(
         spectra_kernel,
         out_shape=jax.ShapeDtypeStruct((16, SENT_ROWS, 128), BF),
         in_specs=[far] * 3,
-        out_specs=near,
+        out_specs=far,
         scratch_shapes=[
+            pltpu.VMEM((16, SENT_ROWS, 128), BF),
             pltpu.VMEM((WIN, CH), jnp.int32),
             pltpu.VMEM((CH, WIN, SEG), BF),
             pltpu.VMEM((512, SEG), BF),
             pltpu.VMEM((PARTS, 2 * WIDE, SEG), BF),
             pltpu.VMEM((SEG // 128, CH * STRIDE + 32, 128), F32),
-            pltpu.VMEM((2, 4, WIDE, 128), F32),
-            pltpu.VMEM((4, WIDE + 16, 128), F32),
+            pltpu.VMEM((PARTS, 2, 4, WIDE, 128), F32),
+            pltpu.VMEM((PARTS, 4, WIDE + 16, 128), F32),
             pltpu.SemaphoreType.DMA((9 + PARTS,)),
+            pltpu.SemaphoreType.DMA((4,)),
         ],
         compiler_params=pltpu.CompilerParams(vmem_limit_bytes=62 << 20),
         cost_estimate=pl.CostEstimate(

time: 108 us -> 108 us (level)
  no operation moved by 1% of the time
where the time goes in v4:
time: 108 us; the launch traced here: 107 us
  waiting for transfers between devices  46.4 us (43%)
  blocking collectives  23.8 us (22%)
  Pallas kernels  20.1 us (19%)
  starting transfers between devices  12.5 us (12%)
  local copies, waits for them, and re-layouts  4.25 us (4%)
    ppermute x2, waiting for transfers between devices, shifted(): lax.ppermute(value, axes, [(i, (i + steps) % count) for i in range(count)])  35.8 us
    all_to_all x1, blocking collectives, per_device(): own = lax.all_to_all(spectra(records, gap_mask), GROUP, 0, 0, tiled=True)  23.8 us
    all_to_all x2, waiting for transfers between devices, per_device(): lax.all_to_all(cross(p, own, prevs[p]), GROUP, 0, 0, tiled=True)  10.6 us
    all_to_all x2, starting transfers between devices, per_device(): lax.all_to_all(cross(p, own, prevs[p]), GROUP, 0, 0, tiled=True)  9.45 us
    pallas_call x1, Pallas kernels, spectra(): pl.pallas_call(spectra_kernel, out_shape=jax.ShapeDtypeStruct((16, SENT_R...  7.92 us
    pallas_call x2, Pallas kernels, cross(): pl.pallas_call(functools.partial(cross_kernel, part), out_shape=jax.Shape...  5.91 us
    pallas_call x1, Pallas kernels, lag_sums(): pl.pallas_call(lag_kernel, grid=(2,), out_shape=jax.ShapeDtypeStruct((3,...  5.76 us
    unnamed x11, local copies, waits for them, and re-layouts  3.58 us
  transfers between devices with their start and end apart: 4, of which 4 were waited for; matrix products, arithmetic and copies ran while one was open for 1% of the time, Pallas kernels for 6%

profile of v4, /device:TPU:1, one launch (start us, length us, event | category | flops | bytes accessed | tf_op | source)
XLA Modules:
  0.0 107.3 jit_solution(14667307782813441777)
XLA Ops:
  0.0 7.9 %spectra.1 = bf16[16,264,128]{2,1,0:T(8,128)(2,1)} custom-call(bf16[32,16,2048]{2,1,0:T(8,128)(2,1)} %rec_far.1, bf16[2,544,2048]{2,1,0:T(8,128)(2,1)} %constant.32.clone.table_far, s32[16,32]{1,0:T(8,128)} %bitcast.8), custom_call_target="tpu_custom_call" | custom-call | flops 2147483648 | bytes 8388608 | tf_op jit(solution)/shard_map/spectra/pallas_call | solution.py:149
  7.9 23.8 %all_to_all.15.own = bf16[16,264,128]{2,1,0:T(8,128)(2,1)S(1)} all-to-all(bf16[16,264,128]{2,1,0:T(8,128)(2,1)} %spectra.1), channel_id=1, replica_groups=mesh['y'=4,'zh'=4,'x'=4,'zl'=2,'core'=2] {'x','zl','core'}, dimensions={0} | all-to-all | bytes 2162688 | tf_op jit(solution)/shard_map/all_to_all | solution.py:390
  31.8 3.1 %collective-permute-start = (bf16[12,128,128]{2,1,0:T(8,128)(2,1)S(1)}, bf16[12,128,128]{2,1,0:T(8,128)(2,1)S(1)}, u32[]{:S(2)}, u32[]{:S(2)}) collective-permute-start(bf16[12,128,128]{2,1,0:T(8,128)(2,1)S(1)} %slice.25), channel_id=1, source_target_pairs={{0,16},{16,32},{32,48},{48,64},{64,80},{80,96},{96,112},{112,128},... | collective-permute-start | bytes 1179656 | tf_op jit(solution)/shard_map/ppermute | solution.py:382
  34.9 22.3 %collective-permute-done.prev = bf16[12,128,128]{2,1,0:T(8,128)(2,1)S(1)} collective-permute-done((bf16[12,128,128]{2,1,0:T(8,128)(2,1)S(1)}, bf16[12,128,128]{2,1,0:T(8,128)(2,1)S(1)}, u32[]{:S(2)}, u32[]{:S(2)}) %collective-permute-start) | collective-permute-done | bytes 393248 | tf_op jit(solution)/shard_map/ppermute | solution.py:382
  57.2 0.0 collective-permute-start.1
  57.2 2.7 %cross.2 = bf16[16,2,2,16,384]{4,3,2,1,0:T(8,128)(2,1)} custom-call(bf16[16,264,128]{2,1,0:T(8,128)(2,1)S(1)} %all_to_all.15.own, bf16[12,128,128]{2,1,0:T(8,128)(2,1)S(1)} %collective-permute-done.prev), custom_call_target="tpu_custom_call" | custom-call | bytes 1048576 | tf_op jit(solution)/shard_map/cross/pallas_call | solution.py:265
  59.9 4.3 %all-to-all-start.1 = ((bf16[16,2,2,16,384]{4,3,2,1,0:T(8,128)(2,1)}), bf16[16,2,2,16,384]{4,3,2,1,0:T(8,128)(2,1)S(1)}, u32[]{:S(2)}, u32[]{:S(2)}) async-start(bf16[16,2,2,16,384]{4,3,2,1,0:T(8,128)(2,1)} %cross.2), calls=%async_computation.1 | async-start | bytes 1572864 | tf_op jit(solution)/shard_map/all_to_all | solution.py:395
  64.2 13.5 %collective-permute-done.1.prev = bf16[12,136,128]{2,1,0:T(8,128)(2,1)S(1)} collective-permute-done((bf16[12,136,128]{2,1,0:T(8,128)(2,1)S(1)}, bf16[12,136,128]{2,1,0:T(8,128)(2,1)S(1)}, u32[]{:S(2)}, u32[]{:S(2)}) %collective-permute-start.1) | collective-permute-done | bytes 417824 | tf_op jit(solution)/shard_map/ppermute | solution.py:382
  77.7 3.2 %cross.3 = bf16[16,2,2,16,384]{4,3,2,1,0:T(8,128)(2,1)S(1)} custom-call(bf16[16,264,128]{2,1,0:T(8,128)(2,1)S(1)} %all_to_all.15.own, bf16[12,136,128]{2,1,0:T(8,128)(2,1)S(1)} %collective-permute-done.1.prev), custom_call_target="tpu_custom_call" | custom-call | flops 107374182400 | bytes 1048576 | tf_op jit(solution)/shard_map/cross/pallas_call | solution.py:265
  81.0 0.0 copy-start.3
  81.0 0.9 copy-done.3
  81.9 0.0 copy-start.1
  81.9 1.5 %all-to-all-done.1.value = bf16[16,2,2,16,384]{4,3,2,1,0:T(8,128)(2,1)S(1)} async-done(((bf16[16,2,2,16,384]{4,3,2,1,0:T(8,128)(2,1)}), bf16[16,2,2,16,384]{4,3,2,1,0:T(8,128)(2,1)S(1)}, u32[]{:S(2)}, u32[]{:S(2)}) %all-to-all-start.1) | async-done | bytes 786464 | tf_op jit(solution)/shard_map/all_to_all | solution.py:395
  83.3 5.1 %all-to-all-start.2 = ((bf16[16,2,2,16,384]{4,3,2,1,0:T(8,128)(2,1)}), bf16[16,2,2,16,384]{4,3,2,1,0:T(8,128)(2,1)}, u32[]{:S(2)}, u32[]{:S(2)}) async-start(bf16[16,2,2,16,384]{4,3,2,1,0:T(8,128)(2,1)} %copy-done.3), calls=%async_computation.2 | async-start | bytes 1572864 | tf_op jit(solution)/shard_map/all_to_all | solution.py:395
  88.5 0.1 fusion
  88.6 0.1 reshape.7
  88.7 0.1 copy.6
  88.8 0.1 reshape.8
  88.9 0.1 constant_dynamic-slice_fusion
  89.0 0.1 copy.10.own_mask
  89.0 0.1 copy.8
  89.1 0.1 slice.23
  89.2 0.1 copy.9.partner_mask
  89.3 0.0 copy-done.1
  89.3 0.5 turn.1
  89.8 0.0 copy-start
  89.8 1.0 copy-done
  90.8 0.0 copy-start.2
  90.8 0.9 copy-done.2
  91.7 0.0 copy-start.4
  91.7 0.7 copy-done.4
  92.4 9.2 %all-to-all-done.2.second = bf16[16,2,2,16,384]{4,3,2,1,0:T(8,128)(2,1)} async-done(((bf16[16,2,2,16,384]{4,3,2,1,0:T(8,128)(2,1)}), bf16[16,2,2,16,384]{4,3,2,1,0:T(8,128)(2,1)}, u32[]{:S(2)}, u32[]{:S(2)}) %all-to-all-start.2) | async-done | bytes 786464 | tf_op jit(solution)/shard_map/all_to_all | solution.py:395
  101.6 5.8 %lag_sums.1 = bf16[3,8,32,2001]{3,2,1,0:T(8,128)(2,1)} custom-call(bf16[2,768,256]{2,1,0:T(8,128)(2,1)} %copy-done.2, bf16[16,2,2,16,384]{4,3,2,1,0:T(8,128)(2,1)} %all-to-all-done.2.second, f32[768,128]{1,0:T(8,128)} %copy-done.4, bf16[512,1024]{1,0:T(8,128)(2,1)} %copy-done, bf16[512,1024]{1,0:T(8,128)(2,1)} %constant.34.clone.sines), custom_call_target="tpu_custom_call" | custom-call | flops 1573650432 | bytes 7340032 | tf_op jit(solution)/shard_map/lag_sums/pallas_call | solution.py:360
  (5 shorter events, 0.1 us)
Async XLA Ops:
  31.8 25.4 %collective-permute-start = (bf16[12,128,128]{2,1,0:T(8,128)(2,1)S(1)}, bf16[12,128,128]{2,1,0:T(8,128)(2,1)S(1)}, u32[]{:S(2)}, u32[]{:S(2)}) collective-permute-start(bf16[12,128,128]{2,1,0:T(8,128)(2,1)S(1)} %slice.25), channel_id=1, source_target_pairs={{0,16},{16,32},{32,48},{48,64},{64,80},{80,96},{96,112},{112,128},... | collective-permute-start | bytes 1179656 | tf_op jit(solution)/shard_map/ppermute | solution.py:382
  57.2 20.6 %collective-permute-start.1 = (bf16[12,136,128]{2,1,0:T(8,128)(2,1)S(1)}, bf16[12,136,128]{2,1,0:T(8,128)(2,1)S(1)}, u32[]{:S(2)}, u32[]{:S(2)}) collective-permute-start(bf16[12,136,128]{2,1,0:T(8,128)(2,1)S(1)} %slice.24), channel_id=1, source_target_pairs={{0,16},{16,32},{32,48},{48,64},{64,80},{80,96},{96,112},{112,128},... | collective-permute-start | bytes 1253384 | tf_op jit(solution)/shard_map/ppermute | solution.py:382
  59.9 23.4 %all-to-all-start.1 = ((bf16[16,2,2,16,384]{4,3,2,1,0:T(8,128)(2,1)}), bf16[16,2,2,16,384]{4,3,2,1,0:T(8,128)(2,1)S(1)}, u32[]{:S(2)}, u32[]{:S(2)}) async-start(bf16[16,2,2,16,384]{4,3,2,1,0:T(8,128)(2,1)} %cross.2), calls=%async_computation.1 | async-start | bytes 1572864 | tf_op jit(solution)/shard_map/all_to_all | solution.py:395
  81.0 0.9 copy-start.3
  81.9 7.4 %copy-start.1 = (bf16[512,1024]{1,0:T(8,128)(2,1)S(1)}, bf16[512,1024]{1,0:T(8,128)(2,1)}, u32[]{:S(2)}) copy-start(bf16[512,1024]{1,0:T(8,128)(2,1)} %constant.33.clone.table_far) | copy-start | bytes 3145732
  83.3 18.2 %all-to-all-start.2 = ((bf16[16,2,2,16,384]{4,3,2,1,0:T(8,128)(2,1)}), bf16[16,2,2,16,384]{4,3,2,1,0:T(8,128)(2,1)}, u32[]{:S(2)}, u32[]{:S(2)}) async-start(bf16[16,2,2,16,384]{4,3,2,1,0:T(8,128)(2,1)} %copy-done.3), calls=%async_computation.2 | async-start | bytes 1572864 | tf_op jit(solution)/shard_map/all_to_all | solution.py:395
  89.8 1.0 copy-start
  90.8 0.9 copy-start.2
  91.7 0.7 copy-start.4

commit v5 on v4

--- a/solution.py
+++ b/solution.py
@@ -95,7 +95,7 @@
 
 
 def spectra_kernel(rec_far, table_far, mask_far, out_far, out, mask, rec, rows, table, planes, spec, power, sems, out_sems):
-    chunk = 4
+    chunk = 8
     copies = [
         pltpu.make_async_copy(rec_far.at[c : c + chunk], rec.at[c : c + chunk], sems.at[c // chunk])
         for c in range(0, CH, chunk)

time: 108 us -> 107 us (level)
  no operation moved by 1% of the time
where the time goes in v5:
time: 107 us
  waiting for transfers between devices  46.4 us (43%)
  blocking collectives  23.8 us (22%)
  Pallas kernels  19.4 us (18%)
  starting transfers between devices  12.5 us (12%)
  local copies, waits for them, and re-layouts  4.25 us (4%)
    ppermute x2, waiting for transfers between devices, shifted(): lax.ppermute(value, axes, [(i, (i + steps) % count) for i in range(count)])  35.8 us
    all_to_all x1, blocking collectives, per_device(): own = lax.all_to_all(spectra(records, gap_mask), GROUP, 0, 0, tiled=True)  23.8 us
    all_to_all x2, waiting for transfers between devices, per_device(): lax.all_to_all(cross(p, own, prevs[p]), GROUP, 0, 0, tiled=True)  10.6 us
    all_to_all x2, starting transfers between devices, per_device(): lax.all_to_all(cross(p, own, prevs[p]), GROUP, 0, 0, tiled=True)  9.45 us
    pallas_call x1, Pallas kernels, spectra(): pl.pallas_call(spectra_kernel, out_shape=jax.ShapeDtypeStruct((16, SENT_R...  7.3 us
    pallas_call x2, Pallas kernels, cross(): pl.pallas_call(functools.partial(cross_kernel, part), out_shape=jax.Shape...  5.92 us
    pallas_call x1, Pallas kernels, lag_sums(): pl.pallas_call(lag_kernel, grid=(2,), out_shape=jax.ShapeDtypeStruct((3,...  5.76 us
    unnamed x11, local copies, waits for them, and re-layouts  3.58 us
  transfers between devices with their start and end apart: 4, of which 4 were waited for; matrix products, arithmetic and copies ran while one was open for 1% of the time, Pallas kernels for 6%

profile of v5, /device:TPU:1, one launch (start us, length us, event | category | flops | bytes accessed | tf_op | source)
XLA Modules:
  0.0 106.7 jit_solution(634206110870506999)
XLA Ops:
  0.0 7.3 %spectra.1 = bf16[16,264,128]{2,1,0:T(8,128)(2,1)} custom-call(bf16[32,16,2048]{2,1,0:T(8,128)(2,1)} %rec_far.1, bf16[2,544,2048]{2,1,0:T(8,128)(2,1)} %constant.32.clone.table_far, s32[16,32]{1,0:T(8,128)} %bitcast.8), custom_call_target="tpu_custom_call" | custom-call | flops 2147483648 | bytes 8388608 | tf_op jit(solution)/shard_map/spectra/pallas_call | solution.py:149
  7.3 23.8 %all_to_all.15.own = bf16[16,264,128]{2,1,0:T(8,128)(2,1)S(1)} all-to-all(bf16[16,264,128]{2,1,0:T(8,128)(2,1)} %spectra.1), channel_id=1, replica_groups=mesh['y'=4,'zh'=4,'x'=4,'zl'=2,'core'=2] {'x','zl','core'}, dimensions={0} | all-to-all | bytes 2162688 | tf_op jit(solution)/shard_map/all_to_all | solution.py:390
  31.2 3.1 %collective-permute-start = (bf16[12,128,128]{2,1,0:T(8,128)(2,1)S(1)}, bf16[12,128,128]{2,1,0:T(8,128)(2,1)S(1)}, u32[]{:S(2)}, u32[]{:S(2)}) collective-permute-start(bf16[12,128,128]{2,1,0:T(8,128)(2,1)S(1)} %slice.25), channel_id=1, source_target_pairs={{0,16},{16,32},{32,48},{48,64},{64,80},{80,96},{96,112},{112,128},... | collective-permute-start | bytes 1179656 | tf_op jit(solution)/shard_map/ppermute | solution.py:382
  34.3 22.3 %collective-permute-done.prev = bf16[12,128,128]{2,1,0:T(8,128)(2,1)S(1)} collective-permute-done((bf16[12,128,128]{2,1,0:T(8,128)(2,1)S(1)}, bf16[12,128,128]{2,1,0:T(8,128)(2,1)S(1)}, u32[]{:S(2)}, u32[]{:S(2)}) %collective-permute-start) | collective-permute-done | bytes 393248 | tf_op jit(solution)/shard_map/ppermute | solution.py:382
  56.6 0.0 collective-permute-start.1
  56.6 2.7 %cross.2 = bf16[16,2,2,16,384]{4,3,2,1,0:T(8,128)(2,1)} custom-call(bf16[16,264,128]{2,1,0:T(8,128)(2,1)S(1)} %all_to_all.15.own, bf16[12,128,128]{2,1,0:T(8,128)(2,1)S(1)} %collective-permute-done.prev), custom_call_target="tpu_custom_call" | custom-call | bytes 1048576 | tf_op jit(solution)/shard_map/cross/pallas_call | solution.py:265
  59.3 4.3 %all-to-all-start.1 = ((bf16[16,2,2,16,384]{4,3,2,1,0:T(8,128)(2,1)}), bf16[16,2,2,16,384]{4,3,2,1,0:T(8,128)(2,1)S(1)}, u32[]{:S(2)}, u32[]{:S(2)}) async-start(bf16[16,2,2,16,384]{4,3,2,1,0:T(8,128)(2,1)} %cross.2), calls=%async_computation.1 | async-start | bytes 1572864 | tf_op jit(solution)/shard_map/all_to_all | solution.py:395
  63.6 13.5 %collective-permute-done.1.prev = bf16[12,136,128]{2,1,0:T(8,128)(2,1)S(1)} collective-permute-done((bf16[12,136,128]{2,1,0:T(8,128)(2,1)S(1)}, bf16[12,136,128]{2,1,0:T(8,128)(2,1)S(1)}, u32[]{:S(2)}, u32[]{:S(2)}) %collective-permute-start.1) | collective-permute-done | bytes 417824 | tf_op jit(solution)/shard_map/ppermute | solution.py:382
  77.1 3.2 %cross.3 = bf16[16,2,2,16,384]{4,3,2,1,0:T(8,128)(2,1)S(1)} custom-call(bf16[16,264,128]{2,1,0:T(8,128)(2,1)S(1)} %all_to_all.15.own, bf16[12,136,128]{2,1,0:T(8,128)(2,1)S(1)} %collective-permute-done.1.prev), custom_call_target="tpu_custom_call" | custom-call | flops 107374182400 | bytes 1048576 | tf_op jit(solution)/shard_map/cross/pallas_call | solution.py:265
  80.3 0.0 copy-start.3
  80.4 0.9 copy-done.3
  81.3 0.0 copy-start.1
  81.3 1.5 %all-to-all-done.1.value = bf16[16,2,2,16,384]{4,3,2,1,0:T(8,128)(2,1)S(1)} async-done(((bf16[16,2,2,16,384]{4,3,2,1,0:T(8,128)(2,1)}), bf16[16,2,2,16,384]{4,3,2,1,0:T(8,128)(2,1)S(1)}, u32[]{:S(2)}, u32[]{:S(2)}) %all-to-all-start.1) | async-done | bytes 786464 | tf_op jit(solution)/shard_map/all_to_all | solution.py:395
  82.7 5.1 %all-to-all-start.2 = ((bf16[16,2,2,16,384]{4,3,2,1,0:T(8,128)(2,1)}), bf16[16,2,2,16,384]{4,3,2,1,0:T(8,128)(2,1)}, u32[]{:S(2)}, u32[]{:S(2)}) async-start(bf16[16,2,2,16,384]{4,3,2,1,0:T(8,128)(2,1)} %copy-done.3), calls=%async_computation.2 | async-start | bytes 1572864 | tf_op jit(solution)/shard_map/all_to_all | solution.py:395
  87.9 0.1 fusion
  88.0 0.1 reshape.7
  88.1 0.1 copy.6
  88.2 0.1 reshape.8
  88.3 0.1 constant_dynamic-slice_fusion
  88.4 0.1 copy.10.own_mask
  88.4 0.1 copy.8
  88.5 0.1 slice.23
  88.6 0.1 copy.9.partner_mask
  88.7 0.0 copy-done.1
  88.7 0.5 turn.1
  89.2 0.0 copy-start
  89.2 1.0 copy-done
  90.2 0.0 copy-start.2
  90.2 0.9 copy-done.2
  91.1 0.0 copy-start.4
  91.1 0.7 copy-done.4
  91.8 9.2 %all-to-all-done.2.second = bf16[16,2,2,16,384]{4,3,2,1,0:T(8,128)(2,1)} async-done(((bf16[16,2,2,16,384]{4,3,2,1,0:T(8,128)(2,1)}), bf16[16,2,2,16,384]{4,3,2,1,0:T(8,128)(2,1)}, u32[]{:S(2)}, u32[]{:S(2)}) %all-to-all-start.2) | async-done | bytes 786464 | tf_op jit(solution)/shard_map/all_to_all | solution.py:395
  101.0 5.8 %lag_sums.1 = bf16[3,8,32,2001]{3,2,1,0:T(8,128)(2,1)} custom-call(bf16[2,768,256]{2,1,0:T(8,128)(2,1)} %copy-done.2, bf16[16,2,2,16,384]{4,3,2,1,0:T(8,128)(2,1)} %all-to-all-done.2.second, f32[768,128]{1,0:T(8,128)} %copy-done.4, bf16[512,1024]{1,0:T(8,128)(2,1)} %copy-done, bf16[512,1024]{1,0:T(8,128)(2,1)} %constant.34.clone.sines), custom_call_target="tpu_custom_call" | custom-call | flops 1573650432 | bytes 7340032 | tf_op jit(solution)/shard_map/lag_sums/pallas_call | solution.py:360
  (5 shorter events, 0.1 us)
Async XLA Ops:
  31.2 25.4 %collective-permute-start = (bf16[12,128,128]{2,1,0:T(8,128)(2,1)S(1)}, bf16[12,128,128]{2,1,0:T(8,128)(2,1)S(1)}, u32[]{:S(2)}, u32[]{:S(2)}) collective-permute-start(bf16[12,128,128]{2,1,0:T(8,128)(2,1)S(1)} %slice.25), channel_id=1, source_target_pairs={{0,16},{16,32},{32,48},{48,64},{64,80},{80,96},{96,112},{112,128},... | collective-permute-start | bytes 1179656 | tf_op jit(solution)/shard_map/ppermute | solution.py:382
  56.6 20.6 %collective-permute-start.1 = (bf16[12,136,128]{2,1,0:T(8,128)(2,1)S(1)}, bf16[12,136,128]{2,1,0:T(8,128)(2,1)S(1)}, u32[]{:S(2)}, u32[]{:S(2)}) collective-permute-start(bf16[12,136,128]{2,1,0:T(8,128)(2,1)S(1)} %slice.24), channel_id=1, source_target_pairs={{0,16},{16,32},{32,48},{48,64},{64,80},{80,96},{96,112},{112,128},... | collective-permute-start | bytes 1253384 | tf_op jit(solution)/shard_map/ppermute | solution.py:382
  59.3 23.5 %all-to-all-start.1 = ((bf16[16,2,2,16,384]{4,3,2,1,0:T(8,128)(2,1)}), bf16[16,2,2,16,384]{4,3,2,1,0:T(8,128)(2,1)S(1)}, u32[]{:S(2)}, u32[]{:S(2)}) async-start(bf16[16,2,2,16,384]{4,3,2,1,0:T(8,128)(2,1)} %cross.2), calls=%async_computation.1 | async-start | bytes 1572864 | tf_op jit(solution)/shard_map/all_to_all | solution.py:395
  80.3 0.9 copy-start.3
  81.3 7.5 %copy-start.1 = (bf16[512,1024]{1,0:T(8,128)(2,1)S(1)}, bf16[512,1024]{1,0:T(8,128)(2,1)}, u32[]{:S(2)}) copy-start(bf16[512,1024]{1,0:T(8,128)(2,1)} %constant.33.clone.table_far) | copy-start | bytes 3145732
  82.7 18.2 %all-to-all-start.2 = ((bf16[16,2,2,16,384]{4,3,2,1,0:T(8,128)(2,1)}), bf16[16,2,2,16,384]{4,3,2,1,0:T(8,128)(2,1)}, u32[]{:S(2)}, u32[]{:S(2)}) async-start(bf16[16,2,2,16,384]{4,3,2,1,0:T(8,128)(2,1)} %copy-done.3), calls=%async_computation.2 | async-start | bytes 1572864 | tf_op jit(solution)/shard_map/all_to_all | solution.py:395
  89.2 1.0 copy-start
  90.2 0.9 copy-start.2
  91.1 0.7 copy-start.4
